TPU v7x, 128 devices: a whole 4x4x4 slice. The times are simulated.
128 devices in a mesh: lat: 64 (over z, y, x_hi, core), lon: 2 (over x_lo).
Axes of the slice: x: 4 (x_hi: 2, x_lo: 2; x = x_hi * 2 + x_lo), y: 4, z: 4, core: 2. Of those that a mesh axis runs over, the one named last changes fastest.
Arguments:
- state: bfloat16 [73, 512, 1024], P(None, 'lat', 'lon'), may hold values from -6 to 6
- in_weight: bfloat16 [73, 384], replicated, may hold values from -0.75 to 0.75
- in_bias: float32 [384], replicated, may hold values from -3 to 3
- out_weight: bfloat16 [384, 384], replicated, may hold values from -0.3125 to 0.3125
- out_bias: float32 [384], replicated, may hold values from -3 to 3
- legendre: bfloat16 [256, 2, 512, 512], P('lat', None, 'lon'), may hold values from -0.25 to 0.25
Outputs:
- coefficients: bfloat16 [256, 2, 512, 2, 384], P('lat', None, None, None, 'lon')
All inputs are finite; a program needn't handle non-finite values.
Results may differ from a plain program's by a relative error of at most 0.0056.
Values may be sent and summed in bfloat16 or wider, within the bound.
No kernel may reach another device: no remote copies, remote signals or barrier semaphores. Data moves between devices by JAX's collectives and lax.ppermute only.
A program may use at most 64 MiB of HBM per device.

v0:
```python
import jax
import jax.numpy as jnp
from jax import lax
from jax.sharding import PartitionSpec as P

NLON = 1024
MM = 512


def order_of(positions):
    pair_index = positions // 2
    member = positions % 2
    return jnp.where(member == 0, pair_index, MM - 1 - pair_index)


def dft_table():
    orders = order_of(jnp.arange(MM, dtype=jnp.int32))
    columns = jnp.arange(NLON, dtype=jnp.int32)
    phases = columns[:, None] * orders[None, :] % NLON
    angles = phases.astype(jnp.float32) * jnp.float32(2.0 * jnp.pi / NLON)
    factor = jnp.float32(1.0) / jnp.sqrt(jnp.float32(NLON))
    tables = jnp.stack([jnp.cos(angles), -jnp.sin(angles)], axis=1) * factor
    return tables.astype(jnp.bfloat16)


def encode(lat_rows, in_weight, in_bias, out_weight, out_bias):
    hidden = jnp.einsum("cab,ch->hab", lat_rows, in_weight, preferred_element_type=jnp.float32)
    hidden = jax.nn.gelu(hidden + in_bias[:, None, None], approximate=False).astype(jnp.bfloat16)
    features = jnp.einsum("hab,hd->dab", hidden, out_weight, preferred_element_type=jnp.float32)
    return (features + out_bias[:, None, None]).astype(jnp.bfloat16)


def transform(features):
    spectra = jnp.einsum("can,nrq->qarc", features, dft_table(), preferred_element_type=jnp.float32)
    return spectra.astype(jnp.bfloat16)


def shards(state, in_weight, in_bias, out_weight, out_bias, legendre):
    features = encode(state, in_weight, in_bias, out_weight, out_bias)
    features = lax.all_to_all(features, "lon", split_axis=0, concat_axis=2, tiled=True)
    spectra = transform(features)
    spectra = lax.all_to_all(spectra, "lat", split_axis=0, concat_axis=1, tiled=True)
    slots = spectra.shape[0]
    channels = spectra.shape[3]
    positions = lax.axis_index("lat") * slots + jnp.arange(slots, dtype=jnp.int32)
    orders = order_of(positions)
    degrees = jnp.arange(MM, dtype=jnp.int32)
    piece = lax.all_gather(legendre, "lon", axis=2, tiled=True)
    count = piece.shape[2]
    weights = piece.reshape(slots, count, MM)
    kept_part = jnp.where(
        degrees[None, None, :] >= orders[:, None, None], weights, jnp.zeros_like(weights)
    )
    coefficients = jnp.einsum(
        "skl,skrc->slrc", kept_part, spectra, preferred_element_type=jnp.float32
    )
    return coefficients.astype(jnp.bfloat16).reshape(slots // 2, 2, MM, 2, channels)


def solution(mesh):
    return jax.shard_map(
        shards,
        mesh=mesh,
        in_specs=(P(None, "lat", "lon"), P(), P(), P(), P(), P("lat", None, "lon", None)),
        out_specs=P("lat", None, None, None, "lon"),
        check_vma=False,
    )
```

profile of v0, /device:TPU:1, one launch (start us, length us, event | category | flops | bytes accessed | tf_op | source)
XLA Modules:
  0.0 213.9 jit_solution(14777640400909605020)
XLA Ops:
  6.5 0.0 copy-start
  6.5 1.1 copy-done
  7.6 0.0 copy-start.1
  7.6 0.0 copy-start.2
  7.6 0.0 copy-start.3
  7.6 4.1 %fusion.25 = (u8[384,512]{1,0:T(8,128)(4,1)S(1)}, u8[384,512]{1,0:T(8,128)(4,1)S(1)}, f32[384,8,512]{2,0,1:T(8,128)S(1)}) fusion(f32[384]{0:T(512)} %param.8, bf16[73,8,512]{2,1,0:T(8,128)(2,1)S(1)} %copy-done, bf16[73,384]{1,0:T(8,128)(2,1)} %param.7), kind=kOutput, calls=%fused_computation.43 | convolution fusion | flops 251265024 | bytes 7340288 | tf_op jit(solution)/shard_map/cab,ch->hab/dot_general | solution.py:27
  11.8 0.0 copy-done.1
  11.8 0.0 copy-done.2
  11.8 0.0 copy-done.3
  11.8 17.2 %fusion.10 = bf16[384,8,512]{0,2,1:T(8,128)(2,1)} fusion(f32[384]{0:T(512)S(1)} %copy-done.2, f32[384,8,512]{2,0,1:T(8,128)S(1)} %get-tuple-element.9, f32[384]{0:T(512)S(1)} %copy-done.3, u8[384,512]{1,0:T(8,128)(4,1)S(1)} %get-tuple-element.6, u8[384,512]{1,0:T(8,128)(4,1)S(1)} %get-tuple-element.5, bf16[384,384]{1,0:T(8,128)(2,1)S(1)} %copy-done.1), kind=kOutput, calls=%fused_computation.27 | convolution fusion | flops 1322778624 | bytes 10128384 | tf_op jit(solution)/shard_map/hab,hd->dab/dot_general | solution.py:29
  29.0 5.1 %copy.20 = bf16[384,8,512]{2,1,0:T(8,128)(2,1)} copy(bf16[384,8,512]{0,2,1:T(8,128)(2,1)} %fusion.10) | data formatting | bytes 6291456 | tf_op jit(solution)/shard_map/convert_element_type | solution.py:30
  34.1 5.2 %all-to-all-start = ((bf16[384,8,512]{2,1,0:T(8,128)(2,1)}), bf16[384,8,512]{2,1,0:T(8,128)(2,1)}, u32[]{:S(2)}, u32[]{:S(2)}) async-start(bf16[384,8,512]{2,1,0:T(8,128)(2,1)} %copy.20), calls=%async_computation | async-start | bytes 6291456 | tf_op jit(solution)/shard_map/all_to_all | solution.py:40
  39.3 0.2 all-gather.2.cloned.1.call-start
  39.6 0.5 all-gather.2.cloned.1.call-update
  40.1 9.2 %fusion.26 = (f32[1024,1,512]{2,0,1:T(8,128)S(1)}, f32[1024,1,512]{2,0,1:T(8,128)}) fusion(s32[512]{0:T(512)S(1)} %subtract_select_fusion.1), kind=kLoop, calls=%fused_computation.44 | loop fusion | flops 7864320 | bytes 4196352 | tf_op jit(solution)/shard_map/cos | solution.py:22
  49.3 41.1 %all-to-all-done = bf16[384,8,512]{2,1,0:T(8,128)(2,1)} async-done(((bf16[384,8,512]{2,1,0:T(8,128)(2,1)}), bf16[384,8,512]{2,1,0:T(8,128)(2,1)}, u32[]{:S(2)}, u32[]{:S(2)}) %all-to-all-start) | async-done | bytes 3145760 | tf_op jit(solution)/shard_map/all_to_all | solution.py:40
  90.4 6.8 %copy.21 = bf16[192,8,2,512]{3,2,0,1:T(2,128)(2,1)} copy(bf16[192,8,2,512]{3,1,0,2:T(8,128)(2,1)} %bitcast.7) | data formatting | bytes 6291456 | tf_op jit(solution)/shard_map/all_to_all | solution.py:40
  97.2 6.1 %reshape.187 = bf16[192,8,1024,1]{2,0,1,3:T(8,128)(2,1)} reshape(bf16[192,8,2,512]{3,2,0,1:T(2,128)(2,1)} %copy.21) | data formatting | bytes 6291456 | tf_op jit(solution)/shard_map/all_to_all | solution.py:40
  103.2 7.7 %convert_bitcast_fusion = bf16[512,8,2,192]{0,3,1,2:T(8,128)(2,1)} fusion(bf16[192,8,1024,1]{2,0,1,3:T(8,128)(2,1)} %reshape.187, f32[1024,1,512]{2,0,1:T(8,128)} %get-tuple-element.8, f32[1024,1,512]{2,0,1:T(8,128)S(1)} %get-tuple-element.7), kind=kOutput, calls=%fused_computation.28 | convolution fusion | flops 3225944064 | bytes 10485760 | tf_op jit(solution)/shard_map/can,nrq->qarc/dot_general | solution.py:34
  110.9 7.7 %copy.22 = bf16[512,8,2,192]{3,1,2,0:T(8,128)(2,1)} copy(bf16[512,8,2,192]{0,3,1,2:T(8,128)(2,1)} %convert_bitcast_fusion) | data formatting | bytes 6291456 | tf_op jit(solution)/shard_map/convert_element_type | solution.py:35
  118.6 17.5 %all-to-all-start.1 = ((bf16[512,8,2,192]{3,1,2,0:T(8,128)(2,1)}), bf16[512,8,2,192]{3,1,2,0:T(8,128)(2,1)}, u32[]{:S(2)}, u32[]{:S(2)}) async-start(bf16[512,8,2,192]{3,1,2,0:T(8,128)(2,1)} %copy.22), calls=%async_computation.1 | async-start | bytes 8388608 | tf_op jit(solution)/shard_map/all_to_all | solution.py:42
  136.1 0.1 iota_compare_fusion
  136.2 0.0 all-gather.2.cloned.1.call-done
  136.2 4.5 %bitcast_select_fusion = bf16[8,512,512]{2,1,0:T(8,128)(2,1)} fusion(bf16[4,2,512,512]{3,2,1,0:T(8,128)(2,1)} %all-gather.2.cloned.1.call-done, pred[8,512]{1,0:T(8,128)(4,1)S(1)} %iota_compare_fusion), kind=kLoop, calls=%fused_computation.25 | loop fusion | flops 2097152 | bytes 8392704 | tf_op jit(solution)/shard_map/jit(_where)/select_n | solution.py:51
  140.7 48.7 %all-to-all-done.1 = bf16[512,8,2,192]{3,1,2,0:T(8,128)(2,1)} async-done(((bf16[512,8,2,192]{3,1,2,0:T(8,128)(2,1)}), bf16[512,8,2,192]{3,1,2,0:T(8,128)(2,1)}, u32[]{:S(2)}, u32[]{:S(2)}) %all-to-all-start.1) | async-done | bytes 3145760 | tf_op jit(solution)/shard_map/all_to_all | solution.py:42
  189.3 4.5 %copy.32 = bf16[8,64,8,2,192]{4,2,1,3,0:T(8,128)(2,1)} copy(bf16[8,64,8,2,192]{4,2,3,0,1:T(8,128)(2,1)} %bitcast.10) | data formatting | bytes 6291456 | tf_op jit(solution)/shard_map/all_to_all | solution.py:42
  193.9 6.2 %copy.24 = bf16[8,512,2,192]{1,3,2,0:T(8,128)(2,1)} copy(bf16[8,512,2,192]{3,1,2,0:T(8,128)(2,1)} %bitcast.38) | data formatting | bytes 6291456 | tf_op jit(solution)/shard_map/all_to_all | solution.py:42
  200.0 4.9 %fusion.74 = f32[8,512,384]{1,2,0:S(1)} fusion(bf16[8,512,384]{1,2,0:T(8,128)(2,1)} %bitcast.37, bf16[8,512,512]{2,1,0:T(8,128)(2,1)} %bitcast_select_fusion), kind=kOutput, calls=%fused_computation.104 | convolution fusion | flops 1610612736 | bytes 13631488
  205.0 2.1 convert_element_type.44
  (2 shorter events, 0.0 us)
Async XLA Ops:
  6.5 1.1 copy-start
  7.6 4.2 %copy-start.1 = (bf16[384,384]{1,0:T(8,128)(2,1)S(1)}, bf16[384,384]{1,0:T(8,128)(2,1)}, u32[]{:S(2)}) copy-start(bf16[384,384]{1,0:T(8,128)(2,1)} %param.9) | copy-start | bytes 884740
  7.6 4.2 %copy-start.2 = (f32[384]{0:T(512)S(1)}, f32[384]{0:T(512)}, u32[]{:S(2)}) copy-start(f32[384]{0:T(512)} %param.10) | copy-start | bytes 4612
  7.6 4.2 %copy-start.3 = (f32[384]{0:T(512)S(1)}, f32[384]{0:T(512)}, u32[]{:S(2)}) copy-start(f32[384]{0:T(512)} %param.8) | copy-start | bytes 4612
  34.1 56.3 %all-to-all-start = ((bf16[384,8,512]{2,1,0:T(8,128)(2,1)}), bf16[384,8,512]{2,1,0:T(8,128)(2,1)}, u32[]{:S(2)}, u32[]{:S(2)}) async-start(bf16[384,8,512]{2,1,0:T(8,128)(2,1)} %copy.20), calls=%async_computation | async-start | bytes 6291456 | tf_op jit(solution)/shard_map/all_to_all | solution.py:40
  39.3 96.9 %all-gather.2.cloned.1.call-start = ((), (), s32[]{:S(2)}) async-start(), calls=%async_computation.2 | async-start | bytes 6291456 | tf_op jit(solution)/shard_map/all_gather | solution.py:48
  118.6 70.7 %all-to-all-start.1 = ((bf16[512,8,2,192]{3,1,2,0:T(8,128)(2,1)}), bf16[512,8,2,192]{3,1,2,0:T(8,128)(2,1)}, u32[]{:S(2)}, u32[]{:S(2)}) async-start(bf16[512,8,2,192]{3,1,2,0:T(8,128)(2,1)} %copy.22), calls=%async_computation.1 | async-start | bytes 8388608 | tf_op jit(solution)/shard_map/all_to_all | solution.py:42
Sparse Core Ops, SparseCore 0:
  41.8 79.7 all-gather.1
where the time goes:
time: 216 us; the launch traced here: 214 us
  waiting for transfers between devices  90.3 us (42%)
  local copies, waits for them, and re-layouts  37.4 us (17%)
  matrix products  33.9 us (16%)
  starting transfers between devices  22.9 us (11%)
  other arithmetic  15.9 us (7%)
  between operations  13.5 us (6%)
    all_to_all x1, waiting for transfers between devices, shards(): lax.all_to_all(spectra, 'lat', split_axis=0, concat_axis=1, tiled=True)  48.7 us
    all_to_all x1, waiting for transfers between devices, shards(): lax.all_to_all(features, 'lon', split_axis=0, concat_axis=2, tiled=True)  41.1 us
    all_to_all x1, starting transfers between devices, shards(): lax.all_to_all(spectra, 'lat', split_axis=0, concat_axis=1, tiled=True)  17.5 us
    dot_general x1, matrix products, encode(): jnp.einsum('hab,hd->dab', hidden, out_weight, preferred_element_type=jnp....  17.2 us
    all_to_all x2, local copies, waits for them, and re-layouts, shards(): lax.all_to_all(features, 'lon', split_axis=0, concat_axis=2, tiled=True)  12.9 us
    all_to_all x2, local copies, waits for them, and re-layouts, shards(): lax.all_to_all(spectra, 'lat', split_axis=0, concat_axis=1, tiled=True)  10.7 us
    cos x1, other arithmetic, dft_table(): tables = jnp.stack([jnp.cos(angles), -jnp.sin(angles)], axis=1) * factor  9.22 us
    convert_element_type x1, local copies, waits for them, and re-layouts, transform(): return spectra.astype(jnp.bfloat16)  7.69 us
  transfers between devices with their start and end apart: 3, of which 2 were waited for; matrix products, arithmetic and copies ran while one was open for 20% of the time, Pallas kernels for 0%

commit v1 on v0

v1 whole, which is shorter than its diff:
```python
import functools

import jax
import jax.numpy as jnp
import numpy as np
from jax import lax
from jax.experimental import pallas as pl
from jax.experimental.pallas import tpu as pltpu
from jax.sharding import PartitionSpec as P

NLON = 1024
HALF = NLON // 2
MM = 512
C = 384
CH = C // 2
OWNERS = 64
PAIRS = 4
LATS = 4
LANE = 128
TILES = MM // LANE
KEPT = (TILES + 1) * LANE
ALL = ("lat", "lon")
MIB = 1 << 20


def dft_tables():
    owner = np.arange(OWNERS)
    columns = np.arange(HALF)
    even, odd = [], []
    for pair in range(PAIRS):
        for member in range(2):
            index = PAIRS * owner + pair
            order = index if member == 0 else MM - 1 - index
            phase = (order[:, None] * columns[None, :]) % NLON
            angle = phase * (2.0 * np.pi / NLON)
            rows = np.stack([np.cos(angle), -np.sin(angle)]) / np.sqrt(float(NLON))
            (even if order[0] % 2 == 0 else odd).append(rows.reshape(2 * OWNERS, HALF))
    return np.stack([np.concatenate(even), np.concatenate(odd)]).astype(np.float32)


def tile_place(packed_tile, block):
    first = TILES - block
    in_first = packed_tile < first
    return jnp.where(in_first, 0, 1), jnp.where(in_first, block + packed_tile, packed_tile - 1)


def order_block():
    return (lax.axis_index("lat") * PAIRS) // LANE


def pack_kernel(legendre_ref, packed_ref):
    block = order_block()
    for tile in range(TILES + 1):
        member, source = tile_place(tile, block)
        start = pl.multiple_of(source * LANE, LANE)
        packed_ref[0, :, tile * LANE:(tile + 1) * LANE] = legendre_ref[0, member, :, pl.ds(start, LANE)]


def pack(legendre):
    rows = legendre.shape[2]
    return pl.pallas_call(
        pack_kernel,
        grid=(PAIRS,),
        in_specs=[pl.BlockSpec((1, 2, rows, MM), lambda i: (i, 0, 0, 0))],
        out_specs=pl.BlockSpec((1, rows, KEPT), lambda i: (i, 0, 0)),
        out_shape=jax.ShapeDtypeStruct((PAIRS, rows, KEPT), jnp.bfloat16),
        cost_estimate=pl.CostEstimate(flops=0, bytes_accessed=4 * MIB, transcendentals=0),
    )(legendre)


def spread_kernel(packed_ref, wide_ref):
    index = lax.axis_index("lat") * PAIRS + pl.program_id(0)
    block = order_block()
    rows = packed_ref.shape[1]
    values = packed_ref[0].astype(jnp.float32).reshape(rows // 8, 8, KEPT)
    lane = lax.broadcasted_iota(jnp.int32, (1, 8, KEPT), 2)
    sub = lax.broadcasted_iota(jnp.int32, (1, 8, KEPT), 1)
    border = (TILES - block) * LANE
    second = lane >= border
    degree = jnp.where(second, lane - LANE, lane + block * LANE)
    order = jnp.where(second, MM - 1 - index, index)
    keep = (degree >= order) & ((sub >= 4) == second)
    swapped = pltpu.roll(values, 4, 1)
    zero = jnp.zeros_like(values)
    upper = jnp.where(keep, jnp.where(second, swapped, values), zero)
    lower = jnp.where(keep, jnp.where(second, values, swapped), zero)
    both = jnp.stack([upper, lower], axis=1)
    wide_ref[0] = both.reshape(2 * rows, KEPT).astype(jnp.bfloat16)


def spread(packed):
    rows = packed.shape[1]
    return pl.pallas_call(
        spread_kernel,
        grid=(PAIRS,),
        in_specs=[pl.BlockSpec((1, rows, KEPT), lambda i: (i, 0, 0))],
        out_specs=pl.BlockSpec((1, 2 * rows, KEPT), lambda i: (i, 0, 0)),
        out_shape=jax.ShapeDtypeStruct((PAIRS, 2 * rows, KEPT), jnp.bfloat16),
        compiler_params=pltpu.CompilerParams(vmem_limit_bytes=32 * MIB),
        cost_estimate=pl.CostEstimate(flops=0, bytes_accessed=4 * MIB, transcendentals=0),
    )(packed)


def gelu(x):
    size = jnp.abs(x)
    t = 1.0 / (1.0 + (0.3275911 * 0.7071067811865476) * size)
    tail = 0.5 * 1.061405429
    for term in (-1.453152027, 1.421413741, -0.284496736, 0.254829592):
        tail = tail * t + 0.5 * term
    tail = tail * t * jnp.exp(-0.5 * x * x)
    return jnp.maximum(x, 0.0) - size * tail


def encode_rows(x, w1, b1, w2, b2):
    contract = (((0,), (0,)), ((), ()))
    hidden = lax.dot_general(x, w1, contract, preferred_element_type=jnp.float32)
    hidden = gelu(hidden + b1).astype(jnp.bfloat16)
    features = jnp.dot(hidden, w2, preferred_element_type=jnp.float32)
    return (features + b2).astype(jnp.bfloat16)


def encode_kernel(x_ref, w1_ref, b1_ref, w2_ref, b2_ref, features_ref):
    row = lax.axis_index("lon") * LATS + pl.program_id(0)
    features_ref[0] = encode_rows(x_ref[row], w1_ref[...], b1_ref[...], w2_ref[...], b2_ref[...])


def whole(array):
    return pl.BlockSpec(array.shape, lambda i: (0,) * array.ndim)


def encode(x, w1, b1, w2, b2):
    return pl.pallas_call(
        encode_kernel,
        grid=(LATS,),
        in_specs=[whole(x), whole(w1), whole(b1), whole(w2), whole(b2)],
        out_specs=pl.BlockSpec((1, HALF, C), lambda i: (i, 0, 0)),
        out_shape=jax.ShapeDtypeStruct((LATS, HALF, C), jnp.bfloat16),
        compiler_params=pltpu.CompilerParams(vmem_limit_bytes=32 * MIB),
        cost_estimate=pl.CostEstimate(flops=2 * LATS * HALF * C * (C + 73), bytes_accessed=4 * MIB,
                                      transcendentals=2 * LATS * HALF * C),
    )(x, w1, b1, w2, b2)


def transform_kernel(x_ref, w1_ref, b1_ref, w2_ref, b2_ref, own_ref, table_ref, out_ref, held):
    lat = pl.program_id(0)
    other = encode_rows(x_ref[0], w1_ref[...], b1_ref[...], w2_ref[...], b2_ref[...]).astype(jnp.float32)
    own = own_ref[0].astype(jnp.float32)
    sign = jnp.where(lax.axis_index("lon") == 0, 1.0, -1.0)
    parts = ((own + other).astype(jnp.bfloat16), (sign * (own - other)).astype(jnp.bfloat16))
    for parity in range(2):
        result = jnp.dot(table_ref[parity], parts[parity], preferred_element_type=jnp.float32)
        for pair in range(PAIRS):
            member = (pair + parity) % 2
            for part in range(2):
                start = (pair * 2 + part) * OWNERS
                rows = pl.ds(member * LATS + lat, OWNERS, stride=2 * LATS)
                for at in range(C // LANE):
                    held[pair * 2 + part, at, rows, :] = (
                        result[start:start + OWNERS, at * LANE:(at + 1) * LANE]
                    )

    @pl.when(lat == LATS - 1)
    def _():
        for pair in range(PAIRS):
            shape = (OWNERS, 2 * LATS, LANE)
            lane = lax.broadcasted_iota(jnp.int32, (OWNERS * 2 * LATS, LANE), 1)
            real_rest = held[pair * 2, 2]
            imag_rest = held[pair * 2 + 1, 2]
            rest = (
                jnp.where(lane < 64, real_rest, pltpu.roll(imag_rest, 64, 1)),
                jnp.where(lane < 64, pltpu.roll(real_rest, 64, 1), imag_rest),
            )
            for side in range(2):
                pieces = (held[pair * 2, side], held[pair * 2 + 1, side], rest[side])
                for at, piece in enumerate(pieces):
                    start = (pair * 3 + at) * LANE
                    out_ref[:, side, :, start:start + LANE] = piece.reshape(shape).astype(jnp.bfloat16)


def transform(x, w1, b1, w2, b2, own, table):
    rows = 2 * LATS
    return pl.pallas_call(
        transform_kernel,
        grid=(LATS,),
        in_specs=[
            pl.BlockSpec((1,) + x.shape[1:], lambda i: (i, 0, 0)),
            whole(w1), whole(b1), whole(w2), whole(b2),
            pl.BlockSpec((1, HALF, C), lambda i: (i, 0, 0)),
            whole(table),
        ],
        out_specs=pl.BlockSpec((OWNERS, 2, rows, PAIRS * C), lambda i: (0, 0, 0, 0)),
        out_shape=jax.ShapeDtypeStruct((OWNERS, 2, rows, PAIRS * C), jnp.bfloat16),
        scratch_shapes=[pltpu.VMEM((2 * PAIRS, C // LANE, OWNERS * rows, LANE), jnp.float32)],
        compiler_params=pltpu.CompilerParams(vmem_limit_bytes=48 * MIB),
        cost_estimate=pl.CostEstimate(flops=2 * LATS * HALF * C * (C + 73 + 2 * MM), bytes_accessed=8 * MIB,
                                      transcendentals=2 * LATS * HALF * C),
    )(x, w1, b1, w2, b2, own, table)


def contract_kernel(spectra_ref, own_ref, other_ref, out_ref):
    half = spectra_ref.shape[0] // 2
    side = lax.axis_index("lon")
    block = order_block()
    dims = (((0,), (0,)), ((), ()))
    mine = spectra_ref[pl.ds(pl.multiple_of(side * half, half), half), :]
    theirs = spectra_ref[pl.ds(pl.multiple_of((1 - side) * half, half), half), :]
    total = lax.dot_general(mine, own_ref[0], dims, preferred_element_type=jnp.float32)
    total += lax.dot_general(theirs, other_ref[0], dims, preferred_element_type=jnp.float32)
    total = total.astype(jnp.bfloat16)
    for tile in range(TILES + 1):
        member, place = tile_place(tile, block)
        lanes = pl.ds(pl.multiple_of(place * LANE, LANE), LANE)
        values = total[:, tile * LANE:(tile + 1) * LANE]
        out_ref[0, member, 0:128, lanes] = values[0:128]
        out_ref[0, member, 192:320, lanes] = values[128:256]
        out_ref[0, member, 128:192, lanes] = values[256:320]
        out_ref[0, member, 320:384, lanes] = values[320:384]
    for tile in range(TILES - 1):
        in_first = tile < block
        member = jnp.where(in_first, 0, 1)
        place = jnp.where(in_first, tile, tile - block)
        lanes = pl.ds(pl.multiple_of(place * LANE, LANE), LANE)
        out_ref[0, member, :, lanes] = jnp.zeros((C, LANE), jnp.bfloat16)


def contract(spectra, own, other):
    rows = spectra.shape[0]
    return pl.pallas_call(
        contract_kernel,
        grid=(PAIRS,),
        in_specs=[
            pl.BlockSpec((rows, C), lambda i: (0, i)),
            pl.BlockSpec((1, rows // 2, KEPT), lambda i: (i, 0, 0)),
            pl.BlockSpec((1, rows // 2, KEPT), lambda i: (i, 0, 0)),
        ],
        out_specs=pl.BlockSpec((1, 2, C, MM), lambda i: (i, 0, 0, 0)),
        out_shape=jax.ShapeDtypeStruct((PAIRS, 2, C, MM), jnp.bfloat16),
        compiler_params=pltpu.CompilerParams(vmem_limit_bytes=48 * MIB),
        cost_estimate=pl.CostEstimate(flops=2 * PAIRS * rows * C * KEPT, bytes_accessed=12 * MIB, transcendentals=0),
    )(spectra, own, other)


def channel_order(array):
    return jnp.concatenate(
        [array[:, 0:128], array[:, 192:320], array[:, 128:192], array[:, 320:384]], axis=1
    )


def shards(state, in_weight, in_bias, out_weight, out_bias, legendre):
    swap = [(0, 1), (1, 0)]
    side = lax.axis_index("lon")
    rows = state.transpose(1, 0, 2)
    sent = lax.dynamic_slice_in_dim(rows, (1 - side) * LATS, LATS, axis=0)
    received = lax.ppermute(sent, "lon", swap)
    weights = (in_weight, in_bias[None, :], channel_order(out_weight), channel_order(out_bias[None, :]))
    own_packed = pack(legendre)
    own = encode(rows, *weights)
    other_packed, received = lax.optimization_barrier((own_packed, received))
    other_packed = lax.ppermute(other_packed, "lon", swap)
    table = jnp.asarray(dft_tables()).astype(jnp.bfloat16)
    spectra = transform(received, *weights, own, table)
    spectra = spectra.reshape(2 * OWNERS * 2 * LATS, PAIRS * C)
    spectra = lax.all_to_all(spectra, ALL, split_axis=0, concat_axis=0, tiled=True)
    result = contract(spectra, spread(own_packed), spread(other_packed))
    return result.reshape(PAIRS, 2, 2, CH, MM).transpose(0, 1, 4, 2, 3)


def solution(mesh):
    return jax.shard_map(
        shards,
        mesh=mesh,
        in_specs=(P(None, "lat", "lon"), P(), P(), P(), P(), P("lat", None, "lon", None)),
        out_specs=P("lat", None, None, None, "lon"),
        check_vma=False,
    )
```

time: 216 us -> 108 us (0.50)
  matrix products: 33.9 us -> 0 us
  waiting for transfers between devices: 90.3 us -> 58.8 us
  local copies, waits for them, and re-layouts: 37.4 us -> 7.48 us
  Pallas kernels: 0 us -> 26.7 us
  other arithmetic: 15.9 us -> 0.18 us
  between operations: 13.5 us -> 0.12 us
  starting transfers between devices: 22.9 us -> 14.6 us
    all_to_all x2 -> x1, waiting for transfers between devices: 89.8 us -> 0.01 us  [shards(): lax.all_to_all(spectra, ALL, split_axis=0, concat_axis=0, tiled=True)]
    ppermute x0 -> x2, waiting for transfers between devices: none -> 58.8 us  [the longest x1 58.8 us: shards(): other_packed = lax.ppermute(other_packed, 'lon', swap)]
    dot_general x3 -> x0, matrix products: 29 us -> none  [the longest x1 17.2 us: encode(): jnp.einsum('hab,hd->dab', hidden, out_weight, preferred_element_type=jnp....]
    pallas_call x0 -> x6, Pallas kernels: none -> 26.7 us  [the longest x1 9.41 us: transform(): pl.pallas_call(transform_kernel, grid=(LATS,), in_specs=[pl.BlockSpec((1,...]
    all_to_all x4 -> x0, local copies, waits for them, and re-layouts: 23.6 us -> none  [the longest x2 12.9 us: shards(): lax.all_to_all(features, 'lon', split_axis=0, concat_axis=2, tiled=True)]
    convert_element_type x2 -> x0, local copies, waits for them, and re-layouts: 12.8 us -> none  [the longest x1 7.69 us: transform(): return spectra.astype(jnp.bfloat16)]
    all_to_all x2 -> x1, starting transfers between devices: 22.7 us -> 11.1 us  [shards(): lax.all_to_all(spectra, ALL, split_axis=0, concat_axis=0, tiled=True)]
    cos x1 -> x0, other arithmetic: 9.22 us -> none  [dft_table(): tables = jnp.stack([jnp.cos(angles), -jnp.sin(angles)], axis=1) * factor]
  transfers between devices with their start and end apart: 3 -> 3, of which waited for: 2 -> 1; matrix products, arithmetic and copies ran while one was open for 20% -> 3% of each run, Pallas kernels for 0% -> 10%
where the time goes in v1:
time: 108 us
  waiting for transfers between devices  58.8 us (54%)
  Pallas kernels  26.7 us (25%)
  starting transfers between devices  14.6 us (14%)
  local copies, waits for them, and re-layouts  7.48 us (7%)
    ppermute x1, waiting for transfers between devices, shards(): other_packed = lax.ppermute(other_packed, 'lon', swap)  58.8 us
    all_to_all x1, starting transfers between devices, shards(): lax.all_to_all(spectra, ALL, split_axis=0, concat_axis=0, tiled=True)  11.1 us
    pallas_call x1, Pallas kernels, transform(): pl.pallas_call(transform_kernel, grid=(LATS,), in_specs=[pl.BlockSpec((1,...  9.41 us
    pallas_call x1, Pallas kernels, contract(): pl.pallas_call(contract_kernel, grid=(PAIRS,), in_specs=[pl.BlockSpec((ro...  6.16 us
    unnamed x11, local copies, waits for them, and re-layouts  4.51 us
    pallas_call x1, Pallas kernels, encode(): pl.pallas_call(encode_kernel, grid=(LATS,), in_specs=[whole(x), whole(w1)...  4.14 us
    pallas_call x1, Pallas kernels, pack(): pl.pallas_call(pack_kernel, grid=(PAIRS,), in_specs=[pl.BlockSpec((1, 2,...  3.7 us
    pallas_call x2, Pallas kernels, spread(): pl.pallas_call(spread_kernel, grid=(PAIRS,), in_specs=[pl.BlockSpec((1, r...  3.31 us
  transfers between devices with their start and end apart: 3, of which 1 were waited for; matrix products, arithmetic and copies ran while one was open for 3% of the time, Pallas kernels for 10%

profile of v1, /device:TPU:1, one launch (start us, length us, event | category | flops | bytes accessed | tf_op | source)
XLA Modules:
  0.0 108.0 jit_solution(7195347395289498906)
XLA Ops:
  0.0 0.0 copy-start.4
  0.0 1.3 %copy.12 = bf16[73,8,512]{2,0,1:T(8,128)(2,1)S(1)} copy(bf16[73,8,512]{2,1,0:T(8,128)(2,1)} %param.7) | data formatting | bytes 1196032 | tf_op args[0]
  1.3 0.0 copy-start.2
  1.3 2.1 %collective-permute-start = (bf16[4,73,512]{2,1,0:T(8,128)(2,1)S(1)}, bf16[4,73,512]{2,1,0:T(8,128)(2,1)S(1)}, u32[]{:S(2)}, u32[]{:S(2)}) collective-permute-start(bf16[4,73,512]{2,1,0:T(8,128)(2,1)S(1)} %dynamic-slice_bitcast_fusion), channel_id=1, source_target_pairs={{0,1},{1,0},{2,3},{3,2},{4,5},{5,4},{6,7},{7,6},{8,9},{9,8},{10,11... | collective-permute-start | bytes 897032 | tf_op jit(solution)/shard_map/ppermute | solution.py:254
  3.4 0.7 broadcast_in_dim.7
  4.1 0.1 fusion.3
  4.2 0.1 fusion.2
  4.3 1.1 fusion
  5.3 1.0 fusion.1
  6.4 0.0 copy-done.4
  6.4 3.7 %shard_map.73.packed_ref = bf16[4,256,640]{2,1,0:T(8,128)(2,1)} custom-call(bf16[4,2,256,512]{3,2,1,0:T(8,128)(2,1)} %legendre_ref.1), custom_call_target="tpu_custom_call" | custom-call | bytes 4194304 | tf_op jit(solution)/shard_map/pallas_call | solution.py:61
  10.1 0.0 copy-start.3
  10.1 0.1 pad_maximum_fusion.1.b2_ref
  10.2 0.1 pad_maximum_fusion.w2_ref
  10.3 0.0 copy-done.2
  10.3 4.1 %shard_map.74.own_ref = bf16[4,512,384]{2,1,0:T(8,128)(2,1)S(1)} custom-call(bf16[8,73,512]{2,1,0:T(8,128)(2,1)S(1)} %bitcast.10, bf16[73,384]{1,0:T(8,128)(2,1)S(1)} %copy-done.2, f32[1,384]{1,0:T(1,128)S(1)} %broadcast_in_dim.6.b1_ref, bf16[384,384]{1,0:T(8,128)(2,1)S(1)} %pad_maximum_fusion.w2_ref, f32[1,384]{1,0:T(1,128)S(1)} %pad_maximum_fusion.1.b2_ref), custom_call_target="tpu_custom_call" | custom-call | flops 718798848 | bytes 4194304 | tf_op jit(solution)/shard_map/pallas_call | solution.py:132
  14.4 0.0 collective-permute-done.x_ref
  14.4 0.0 copy-done.3
  14.5 9.4 %shard_map.75 = bf16[64,2,8,1536]{3,2,1,0:T(8,128)(2,1)} custom-call(bf16[4,73,512]{2,1,0:T(8,128)(2,1)S(1)} %collective-permute-done.x_ref, bf16[73,384]{1,0:T(8,128)(2,1)S(1)} %copy-done.2, f32[1,384]{1,0:T(1,128)S(1)} %broadcast_in_dim.6.b1_ref, bf16[384,384]{1,0:T(8,128)(2,1)S(1)} %pad_maximum_fusion.w2_ref, f32[1,384]{1,0:T(1,128)S(1)} %pad_maximum_fusion.1.b2_ref, ...), custom_call_target="tpu_custom_call" | custom-call | flops 2329411584 | bytes 8388608 | tf_op jit(solution)/shard_map/pallas_call | solution.py:182
  23.9 11.1 %all-to-all-start = ((bf16[128,8,1536]{2,1,0:T(8,128)(2,1)}), bf16[128,8,1536]{2,1,0:T(8,128)(2,1)}, u32[]{:S(2)}, u32[]{:S(2)}) async-start(bf16[128,8,1536]{2,1,0:T(8,128)(2,1)} %bitcast.11), calls=%async_computation | async-start | bytes 6291456 | tf_op jit(solution)/shard_map/all_to_all | solution.py:263
  34.9 1.5 %collective-permute-start.1 = (bf16[4,256,640]{2,1,0:T(8,128)(2,1)}, bf16[4,256,640]{2,1,0:T(8,128)(2,1)S(1)}, u32[]{:S(2)}, u32[]{:S(2)}) collective-permute-start(bf16[4,256,640]{2,1,0:T(8,128)(2,1)} %shard_map.73.packed_ref), channel_id=1, source_target_pairs={{0,1},{1,0},{2,3},{3,2},{4,5},{5,4},{6,7},{7,6},{8,9},{9,8},{10,11... | collective-permute-start | bytes 3932168 | tf_op jit(solution)/shard_map/ppermute | solution.py:259
  36.4 2.6 %shard_map.76.own_ref = bf16[4,512,640]{2,1,0:T(8,128)(2,1)S(1)} custom-call(bf16[4,256,640]{2,1,0:T(8,128)(2,1)} %shard_map.73.packed_ref), custom_call_target="tpu_custom_call" | custom-call | bytes 4194304 | tf_op jit(solution)/shard_map/pallas_call | solution.py:93
  39.0 58.8 %collective-permute-done.1.packed_ref = bf16[4,256,640]{2,1,0:T(8,128)(2,1)S(1)} collective-permute-done((bf16[4,256,640]{2,1,0:T(8,128)(2,1)}, bf16[4,256,640]{2,1,0:T(8,128)(2,1)S(1)}, u32[]{:S(2)}, u32[]{:S(2)}) %collective-permute-start.1) | collective-permute-done | bytes 1310752 | tf_op jit(solution)/shard_map/ppermute | solution.py:259
  97.8 0.7 shard_map.77.other_ref
  98.6 0.0 copy-start
  98.6 1.5 %copy-done = bf16[4,512,640]{2,1,0:T(8,128)(2,1)} copy-done((bf16[4,512,640]{2,1,0:T(8,128)(2,1)}, bf16[4,512,640]{2,1,0:T(8,128)(2,1)S(1)}, u32[]{:S(2)}) %copy-start) | copy-done | bytes 2621464
  100.1 0.0 all-to-all-done
  100.1 0.0 copy-start.1
  100.1 1.7 %copy-done.1 = bf16[4,512,640]{2,1,0:T(8,128)(2,1)S(1)} copy-done((bf16[4,512,640]{2,1,0:T(8,128)(2,1)S(1)}, bf16[4,512,640]{2,1,0:T(8,128)(2,1)}, u32[]{:S(2)}) %copy-start.1) | copy-done | bytes 2621464
  101.8 6.2 %shard_map.78 = bf16[4,2,384,512]{3,2,1,0:T(8,128)(2,1)} custom-call(bf16[1024,1536]{1,0:T(8,128)(2,1)} %bitcast.3.spectra_ref, bf16[4,512,640]{2,1,0:T(8,128)(2,1)S(1)} %shard_map.76.own_ref, bf16[4,512,640]{2,1,0:T(8,128)(2,1)S(1)} %copy-done.1), custom_call_target="tpu_custom_call" | custom-call | flops 2013265920 | bytes 12582912 | tf_op jit(solution)/shard_map/pallas_call | solution.py:228
  (2 shorter events, 0.0 us)
Async XLA Ops:
  0.0 6.4 %copy-start.4 = (f32[384]{0:T(512)S(1)}, f32[384]{0:T(512)}, u32[]{:S(2)}) copy-start(f32[384]{0:T(512)} %param.9) | copy-start | bytes 4612
  1.3 9.0 %copy-start.2 = (bf16[73,384]{1,0:T(8,128)(2,1)S(1)}, bf16[73,384]{1,0:T(8,128)(2,1)}, u32[]{:S(2)}) copy-start(bf16[73,384]{1,0:T(8,128)(2,1)} %w1_ref.3) | copy-start | bytes 168196
  1.3 13.1 %collective-permute-start = (bf16[4,73,512]{2,1,0:T(8,128)(2,1)S(1)}, bf16[4,73,512]{2,1,0:T(8,128)(2,1)S(1)}, u32[]{:S(2)}, u32[]{:S(2)}) collective-permute-start(bf16[4,73,512]{2,1,0:T(8,128)(2,1)S(1)} %dynamic-slice_bitcast_fusion), channel_id=1, source_target_pairs={{0,1},{1,0},{2,3},{3,2},{4,5},{5,4},{6,7},{7,6},{8,9},{9,8},{10,11... | collective-permute-start | bytes 897032 | tf_op jit(solution)/shard_map/ppermute | solution.py:254
  10.1 4.3 %copy-start.3 = (bf16[2,512,512]{2,1,0:T(8,128)(2,1)S(1)}, bf16[2,512,512]{2,1,0:T(8,128)(2,1)}, u32[]{:S(2)}) copy-start(bf16[2,512,512]{2,1,0:T(8,128)(2,1)} %constant.17.table_ref) | copy-start | bytes 3145732
  23.9 76.2 %all-to-all-start = ((bf16[128,8,1536]{2,1,0:T(8,128)(2,1)}), bf16[128,8,1536]{2,1,0:T(8,128)(2,1)}, u32[]{:S(2)}, u32[]{:S(2)}) async-start(bf16[128,8,1536]{2,1,0:T(8,128)(2,1)} %bitcast.11), calls=%async_computation | async-start | bytes 6291456 | tf_op jit(solution)/shard_map/all_to_all | solution.py:263
  34.9 62.9 %collective-permute-start.1 = (bf16[4,256,640]{2,1,0:T(8,128)(2,1)}, bf16[4,256,640]{2,1,0:T(8,128)(2,1)S(1)}, u32[]{:S(2)}, u32[]{:S(2)}) collective-permute-start(bf16[4,256,640]{2,1,0:T(8,128)(2,1)} %shard_map.73.packed_ref), channel_id=1, source_target_pairs={{0,1},{1,0},{2,3},{3,2},{4,5},{5,4},{6,7},{7,6},{8,9},{9,8},{10,11... | collective-permute-start | bytes 3932168 | tf_op jit(solution)/shard_map/ppermute | solution.py:259
  98.6 1.5 %copy-start = (bf16[4,512,640]{2,1,0:T(8,128)(2,1)}, bf16[4,512,640]{2,1,0:T(8,128)(2,1)S(1)}, u32[]{:S(2)}) copy-start(bf16[4,512,640]{2,1,0:T(8,128)(2,1)S(1)} %shard_map.77.other_ref) | copy-start | bytes 7864324
  100.1 1.7 %copy-start.1 = (bf16[4,512,640]{2,1,0:T(8,128)(2,1)S(1)}, bf16[4,512,640]{2,1,0:T(8,128)(2,1)}, u32[]{:S(2)}) copy-start(bf16[4,512,640]{2,1,0:T(8,128)(2,1)} %copy-done) | copy-start | bytes 7864324

commit v2 on v0

v2 whole, which is shorter than its diff:
```python
import jax
import jax.numpy as jnp
import numpy as np
from jax import lax
from jax.experimental import pallas as pl
from jax.experimental.pallas import tpu as pltpu
from jax.sharding import PartitionSpec as P

NLON = 1024
HALF = NLON // 2
MM = 512
C = 384
CH = C // 2
OWNERS = 64
PAIRS = 4
LATS = 8
CHUNK = 384
LANE = 128
TILES = MM // LANE
KEPT = (TILES + 1) * LANE
ALL = ("lat", "lon")
MIB = 1 << 20
SMALL = 16 * MIB
MEDIUM = 24 * MIB


def owner_bit(lat):
    return (lat // 2) % 2


def groups():
    return [[2 * lat + (owner_bit(lat) ^ group) for lat in range(OWNERS)] for group in range(2)]


def my_group():
    return owner_bit(lax.axis_index("lat")) ^ lax.axis_index("lon")


def dft_tables():
    columns = np.arange(HALF)
    tables = []
    for parity in range(2):
        rows = []
        for bit in range(2):
            owner = np.array([lat for lat in range(OWNERS) if owner_bit(lat) == bit])
            for pair in range(PAIRS):
                index = PAIRS * owner + pair
                order = index if (pair + parity) % 2 == 0 else MM - 1 - index
                assert np.all(order % 2 == parity)
                phase = (order[:, None] * columns[None, :]) % NLON
                angle = phase * (2.0 * np.pi / NLON)
                rows += [np.cos(angle), -np.sin(angle)]
        tables.append(np.concatenate(rows) / np.sqrt(float(NLON)))
    return np.stack(tables).astype(np.float32)


def tile_place(packed_tile, block):
    in_first = packed_tile < TILES - block
    return jnp.where(in_first, 0, 1), jnp.where(in_first, block + packed_tile, packed_tile - 1)


def order_block():
    return (lax.axis_index("lat") * PAIRS) // LANE


def channel_order(array):
    pieces = [array[:, 0:128], array[:, 192:320], array[:, 128:192], array[:, 320:384]]
    zero = jnp.concatenate(pieces, axis=1)
    one = jnp.concatenate([pieces[1], pieces[0], pieces[3], pieces[2]], axis=1)
    return jnp.where(my_group() == 0, zero, one)


def encode_rows(x, w1, b1, w2, b2):
    hidden = lax.dot_general(x, w1, (((0,), (0,)), ((), ())), preferred_element_type=jnp.float32)
    hidden = hidden + b1
    hidden = (0.5 * hidden) * (1.0 + lax.erf(hidden * np.float32(np.sqrt(0.5))))
    features = jnp.dot(hidden.astype(jnp.bfloat16), w2, preferred_element_type=jnp.float32)
    return (features + b2).astype(jnp.bfloat16)


def pack_copies(legendre_ref, staged, sems):
    block = order_block()
    copies = []
    for tile in range(TILES + 1):
        member, source = tile_place(tile, block)
        lanes = pl.ds(pl.multiple_of(source * LANE, LANE), LANE)
        copies.append(pltpu.make_async_copy(
            legendre_ref.at[:, member, :, lanes],
            staged.at[:, :, tile * LANE:(tile + 1) * LANE],
            sems.at[tile],
        ))
    return copies


def encode_own_kernel(x_ref, w1_hbm, b1_hbm, w2_hbm, b2_hbm, legendre_ref,
                      features_ref, packed_ref, w1_ref, b1_ref, w2_ref, b2_ref,
                      b1_raw, w2_raw, b2_raw, staged, sems, loaded, sent):
    copies = pack_copies(legendre_ref, staged, sems)
    loads = [
        pltpu.make_async_copy(source, target, loaded.at[at])
        for at, (source, target) in enumerate(
            ((w1_hbm, w1_ref), (b1_hbm, b1_raw), (w2_hbm, w2_raw), (b2_hbm, b2_raw)))
    ]
    for load in loads:
        load.start()
    for copy in copies:
        copy.start()
    for load in loads:
        load.wait()
    b1_ref[...] = b1_raw[...][None, :]
    w2_ref[...] = channel_order(w2_raw[...])
    b2_ref[...] = channel_order(b2_raw[...][None, :])
    encode_kernel(x_ref, w1_ref, b1_ref, w2_ref, b2_ref, features_ref)
    result = pltpu.make_async_copy(staged, packed_ref, sent)
    for copy in copies:
        copy.wait()
    result.start()
    result.wait()


def encode_kernel(x_ref, w1_ref, b1_ref, w2_ref, b2_ref, features_ref):
    for lat in range(LATS):
        features_ref[lat] = encode_rows(x_ref[lat], w1_ref[...], b1_ref[...], w2_ref[...], b2_ref[...])


IN_VMEM = pl.BlockSpec(memory_space=pltpu.VMEM)
IN_HBM = pl.BlockSpec(memory_space=pltpu.HBM)


def encode_cost(lats, lons):
    return pl.CostEstimate(flops=2 * lats * lons * C * (C + 73), bytes_accessed=MIB,
                           transcendentals=lats * lons * C)


def combine(own, theirs):
    own, theirs = own.astype(jnp.float32), theirs.astype(jnp.float32)
    sign = jnp.where(lax.axis_index("lon") == 0, 1.0, -1.0)
    return (own + theirs).astype(jnp.bfloat16), (sign * (own - theirs)).astype(jnp.bfloat16)


def first_kernel(x_ref, w1_ref, b1_ref, w2_ref, b2_ref, own_ref, parts_ref):
    lons = x_ref.shape[2]
    for lat in range(LATS):
        theirs = encode_rows(x_ref[lat], w1_ref[...], b1_ref[...], w2_ref[...], b2_ref[...])
        parts_ref[0, lat], parts_ref[1, lat] = combine(own_ref[lat, :lons], theirs)


def first_lons(x, encoder, own):
    lats, _, lons = x.shape
    return pl.pallas_call(
        first_kernel,
        in_specs=[IN_VMEM] * 6,
        out_specs=IN_VMEM,
        out_shape=pltpu.VMEM((2, lats, lons, C), jnp.bfloat16),
        compiler_params=pltpu.CompilerParams(vmem_limit_bytes=SMALL),
        cost_estimate=encode_cost(lats, lons),
    )(x, *encoder, own)


def encode_own(x, w1, b1, w2, b2, legendre):
    lats, _, lons = x.shape
    pairs, _, rows, _ = legendre.shape
    return pl.pallas_call(
        encode_own_kernel,
        in_specs=[IN_VMEM] + [IN_HBM] * 5,
        out_specs=[IN_VMEM, IN_HBM] + [IN_VMEM] * 4,
        out_shape=[
            pltpu.VMEM((lats, lons, C), jnp.bfloat16),
            pltpu.HBM((pairs, rows, KEPT), jnp.bfloat16),
            pltpu.VMEM(w1.shape, jnp.bfloat16),
            pltpu.VMEM((1, C), jnp.float32),
            pltpu.VMEM(w2.shape, jnp.bfloat16),
            pltpu.VMEM((1, C), jnp.float32),
        ],
        scratch_shapes=[
            pltpu.VMEM(b1.shape, jnp.float32),
            pltpu.VMEM(w2.shape, jnp.bfloat16),
            pltpu.VMEM(b2.shape, jnp.float32),
            pltpu.VMEM((pairs, rows, KEPT), jnp.bfloat16),
            pltpu.SemaphoreType.DMA((TILES + 1,)),
            pltpu.SemaphoreType.DMA((4,)),
            pltpu.SemaphoreType.DMA,
        ],
        compiler_params=pltpu.CompilerParams(vmem_limit_bytes=SMALL),
        cost_estimate=encode_cost(lats, lons),
    )(x, w1, b1, w2, b2, legendre)


def transform_kernel(x_ref, w1_ref, b1_ref, w2_ref, b2_ref, own_ref, first_ref, table_ref, out_ref,
                     rest, held, staged, sems):
    lons = x_ref.shape[2]
    for lat in range(LATS):
        theirs = encode_rows(x_ref[lat], w1_ref[...], b1_ref[...], w2_ref[...], b2_ref[...])
        rest[0, lat], rest[1, lat] = combine(own_ref[lat, HALF - lons:], theirs)
    copies = []
    for block in range(4):
        parity, bit = block // 2, block % 2
        spectra_block(parity, bit, table_ref, (first_ref, rest), held.at[block], staged.at[block])
        copies.append(pltpu.make_async_copy(
            staged.at[block],
            out_ref.at[:, bit, :, :, parity * PAIRS * C:(parity + 1) * PAIRS * C],
            sems.at[block],
        ))
        copies[-1].start()
    for copy in copies:
        copy.wait()


def spectra_block(parity, bit, table_ref, parts, held, staged):
    owners = OWNERS // 2
    left = table_ref[parity, bit * 2 * PAIRS * owners:(bit + 1) * 2 * PAIRS * owners, :]
    for lat in range(LATS):
        right = jnp.concatenate([
            jnp.concatenate([part[parity, lat, :, bit * LANE:(bit + 1) * LANE], part[parity, lat, :, 2 * LANE:]], axis=1)
            for part in parts
        ], axis=0)
        result = jnp.dot(left, right, preferred_element_type=jnp.float32)
        rows = pl.ds(lat, owners, stride=LATS)
        for pair in range(PAIRS):
            for angle in range(2):
                start = (pair * 2 + angle) * owners
                for at in range(2):
                    held[pair, angle, at, rows, :] = result[start:start + owners, at * LANE:(at + 1) * LANE]
    lane = lax.broadcasted_iota(jnp.int32, (owners * LATS, LANE), 1)
    for pair in range(PAIRS):
        real = held[pair, 0, 1]
        imag = held[pair, 1, 1]
        if bit == 0:
            imag = pltpu.roll(imag, 64, 1)
        else:
            real = pltpu.roll(real, 64, 1)
        pieces = (held[pair, 0, 0], held[pair, 1, 0], jnp.where(lane < 64, real, imag))
        for at, piece in enumerate(pieces):
            start = (pair * 3 + at) * LANE
            staged[:, :, :, start:start + LANE] = (
                piece.reshape(owners // 2, 2, LATS, LANE).astype(jnp.bfloat16)
            )


def transform(x, encoder, own, first, table):
    return pl.pallas_call(
        transform_kernel,
        in_specs=[IN_VMEM] * 8,
        out_specs=IN_HBM,
        out_shape=pltpu.HBM((OWNERS // 4, 2, 2, LATS, 2 * PAIRS * C), jnp.bfloat16),
        scratch_shapes=[
            pltpu.VMEM((2, LATS, x.shape[2], C), jnp.bfloat16),
            pltpu.VMEM((4, PAIRS, 2, 2, OWNERS // 2 * LATS, LANE), jnp.float32),
            pltpu.VMEM((4, OWNERS // 4, 2, LATS, PAIRS * C), jnp.bfloat16),
            pltpu.SemaphoreType.DMA((4,)),
        ],
        compiler_params=pltpu.CompilerParams(vmem_limit_bytes=MEDIUM),
        cost_estimate=pl.CostEstimate(flops=2 * LATS * HALF * C * (C // 2 + 2 * MM), bytes_accessed=4 * MIB,
                                      transcendentals=LATS * (HALF - CHUNK) * C),
    )(x, *encoder, own, first, table)


def contract_kernel(even_ref, odd_ref, own_ref, packed_ref, out_ref, other):
    half = own_ref.shape[2]
    side = lax.axis_index("lon")
    block = order_block()
    pair = pl.program_id(0)
    index = lax.axis_index("lat") * PAIRS + pair
    mine = pl.ds(pl.multiple_of(side * half, half), half)
    theirs = pl.ds(pl.multiple_of((1 - side) * half, half), half)
    for tile in range(TILES + 1):
        member, place = tile_place(tile, block)
        lanes = pl.ds(pl.multiple_of(place * LANE, LANE), LANE)
        other[member, :, lanes] = packed_ref[0, :, tile * LANE:(tile + 1) * LANE]
    degree = lax.broadcasted_iota(jnp.int32, (C, MM), 1)
    dims = (((0,), (0,)), ((), ()))
    for parity, spectra_ref in enumerate((even_ref, odd_ref)):
        member = (pair + parity) % 2
        order = jnp.where(member == 0, index, MM - 1 - index)
        values = lax.dot_general(
            spectra_ref[mine, :], own_ref[0, member], dims, preferred_element_type=jnp.float32)
        values += lax.dot_general(
            spectra_ref[theirs, :], other[member], dims, preferred_element_type=jnp.float32)
        values = jnp.where(degree >= order, values, 0.0).astype(jnp.bfloat16)
        out_ref[0, member, 0:128] = values[0:128]
        out_ref[0, member, 192:320] = values[128:256]
        out_ref[0, member, 128:192] = values[256:320]
        out_ref[0, member, 320:384] = values[320:384]


def contract(spectra, legendre, packed):
    rows = spectra.shape[0]
    half = legendre.shape[2]
    spectra = pltpu.with_memory_space_constraint(spectra, pltpu.HBM)
    return pl.pallas_call(
        contract_kernel,
        grid=(PAIRS,),
        in_specs=[
            pl.BlockSpec((rows, C), lambda i: (0, i)),
            pl.BlockSpec((rows, C), lambda i: (0, PAIRS + i)),
            pl.BlockSpec((1, 2, half, MM), lambda i: (i, 0, 0, 0)),
            pl.BlockSpec((1, half, KEPT), lambda i: (i, 0, 0)),
        ],
        out_specs=pl.BlockSpec((1, 2, C, MM), lambda i: (i, 0, 0, 0)),
        out_shape=jax.ShapeDtypeStruct((PAIRS, 2, C, MM), jnp.bfloat16),
        scratch_shapes=[pltpu.VMEM((2, half, MM), jnp.bfloat16)],
        compiler_params=pltpu.CompilerParams(vmem_limit_bytes=SMALL),
        cost_estimate=pl.CostEstimate(flops=4 * PAIRS * rows * C * MM, bytes_accessed=12 * MIB, transcendentals=0),
    )(spectra, spectra, legendre, packed)


def by_lat(flat):
    return flat.reshape(-1, LATS, flat.shape[1]).transpose(1, 0, 2)


def shards(state, in_weight, in_bias, out_weight, out_bias, legendre):
    swap = [(0, 1), (1, 0)]
    flat = state.reshape(-1, HALF)
    received = [lax.ppermute(lons, "lon", swap) for lons in (flat[:, :CHUNK], flat[:, CHUNK:])]
    own, packed, *encoder = encode_own(
        by_lat(flat), *(
            pltpu.with_memory_space_constraint(array, pltpu.HBM)
            for array in (in_weight, in_bias, out_weight, out_bias, legendre)))
    first = first_lons(by_lat(received[0]), encoder, own)
    first, last = lax.optimization_barrier((first, received[1]))
    table = jnp.asarray(dft_tables()).astype(jnp.bfloat16)
    spectra = transform(by_lat(last), encoder, own, first, table)
    packed, spectra = lax.optimization_barrier((packed, spectra))
    packed = lax.ppermute(packed, "lon", swap)
    spectra = spectra.reshape(OWNERS, LATS, 2 * PAIRS * C)
    spectra = lax.all_to_all(spectra, ALL, split_axis=0, concat_axis=0, tiled=True, axis_index_groups=groups())
    result = contract(spectra.reshape(OWNERS * LATS, 2 * PAIRS * C), legendre, packed)
    return result.reshape(PAIRS, 2, 2, CH, MM).transpose(0, 1, 4, 2, 3)


def solution(mesh):
    return jax.shard_map(
        shards,
        mesh=mesh,
        in_specs=(P(None, "lat", "lon"), P(), P(), P(), P(), P("lat", None, "lon", None)),
        out_specs=P("lat", None, None, None, "lon"),
        check_vma=False,
    )
```

time: 216 us -> 84.8 us (0.39)
  waiting for transfers between devices: 90.3 us -> 43.6 us
  local copies, waits for them, and re-layouts: 37.4 us -> 3.33 us
  matrix products: 33.9 us -> 0 us
  Pallas kernels: 0 us -> 21 us
  other arithmetic: 15.9 us -> 0 us
  between operations: 13.5 us -> 0.1 us
  starting transfers between devices: 22.9 us -> 16.4 us
    all_to_all x2 -> x1, waiting for transfers between devices: 89.8 us -> 11.6 us  [shards(): lax.all_to_all(spectra, ALL, split_axis=0, concat_axis=0, tiled=True, axi...]
    ppermute x0 -> x3, waiting for transfers between devices: none -> 32 us  [the longest x1 30.1 us: shards(): packed = lax.ppermute(packed, 'lon', swap)]
    dot_general x3 -> x0, matrix products: 29 us -> none  [the longest x1 17.2 us: encode(): jnp.einsum('hab,hd->dab', hidden, out_weight, preferred_element_type=jnp....]
    all_to_all x4 -> x0, local copies, waits for them, and re-layouts: 23.6 us -> none  [the longest x2 12.9 us: shards(): lax.all_to_all(features, 'lon', split_axis=0, concat_axis=2, tiled=True)]
    pallas_call x0 -> x4, Pallas kernels: none -> 21 us  [the longest x1 6.56 us: transform(): pl.pallas_call(transform_kernel, in_specs=[IN_VMEM] * 8, out_specs=IN_HBM...]
    convert_element_type x2 -> x0, local copies, waits for them, and re-layouts: 12.8 us -> none  [the longest x1 7.69 us: transform(): return spectra.astype(jnp.bfloat16)]
    cos x1 -> x0, other arithmetic: 9.22 us -> none  [dft_table(): tables = jnp.stack([jnp.cos(angles), -jnp.sin(angles)], axis=1) * factor]
    all_to_all x2 -> x1, starting transfers between devices: 22.7 us -> 14.1 us  [shards(): lax.all_to_all(spectra, ALL, split_axis=0, concat_axis=0, tiled=True, axi...]
  transfers between devices with their start and end apart: 3 -> 4, of which waited for: 2 -> 3; matrix products, arithmetic and copies ran while one was open for 20% -> 3% of each run, Pallas kernels for 0% -> 11%
where the time goes in v2:
time: 84.8 us; the launch traced here: 84.4 us
  waiting for transfers between devices  43.6 us (51%)
  Pallas kernels  21 us (25%)
  starting transfers between devices  16.4 us (19%)
  local copies, waits for them, and re-layouts  3.33 us (4%)
    ppermute x1, waiting for transfers between devices, shards(): packed = lax.ppermute(packed, 'lon', swap)  30.1 us
    all_to_all x1, starting transfers between devices, shards(): lax.all_to_all(spectra, ALL, split_axis=0, concat_axis=0, tiled=True, axi...  14.1 us
    all_to_all x1, waiting for transfers between devices, shards(): lax.all_to_all(spectra, ALL, split_axis=0, concat_axis=0, tiled=True, axi...  11.6 us
    pallas_call x1, Pallas kernels, transform(): pl.pallas_call(transform_kernel, in_specs=[IN_VMEM] * 8, out_specs=IN_HBM...  6.56 us
    pallas_call x1, Pallas kernels, contract(): pl.pallas_call(contract_kernel, grid=(PAIRS,), in_specs=[pl.BlockSpec((ro...  5.48 us
    pallas_call x1, Pallas kernels, encode_own(): pl.pallas_call(encode_own_kernel, in_specs=[IN_VMEM] + [IN_HBM] * 5, out_...  5.38 us
    pallas_call x1, Pallas kernels, first_lons(): pl.pallas_call(first_kernel, in_specs=[IN_VMEM] * 6, out_specs=IN_VMEM, o...  3.54 us
    ppermute x2, starting transfers between devices, shards(): lax.ppermute(lons, 'lon', swap)  2.22 us
  transfers between devices with their start and end apart: 4, of which 3 were waited for; matrix products, arithmetic and copies ran while one was open for 3% of the time, Pallas kernels for 11%

profile of v2, /device:TPU:1, one launch (start us, length us, event | category | flops | bytes accessed | tf_op | source)
XLA Modules:
  0.0 84.4 jit_solution(4240305951377017974)
XLA Ops:
  0.0 1.1 %slice.8 = bf16[584,384]{1,0:T(8,128)(2,1)S(1)} slice(bf16[584,512]{1,0:T(8,128)(2,1)} %bitcast.21), slice={[0:584], [0:384]} | slice | bytes 897024 | tf_op jit(solution)/shard_map/slice | solution.py:314
  1.1 2.1 %collective-permute-start = (bf16[584,384]{1,0:T(8,128)(2,1)S(1)}, bf16[584,384]{1,0:T(8,128)(2,1)S(1)}, u32[]{:S(2)}, u32[]{:S(2)}) collective-permute-start(bf16[584,384]{1,0:T(8,128)(2,1)S(1)} %slice.8), channel_id=1, source_target_pairs={{0,1},{1,0},{2,3},{3,2},{4,5},{5,4},{6,7},{7,6},{8,9},{9,8},{10,11... | collective-permute-start | bytes 1345544 | tf_op jit(solution)/shard_map/ppermute | solution.py:314
  3.2 0.9 %slice.9 = bf16[584,128]{1,0:T(8,128)(2,1)S(1)} slice(bf16[584,512]{1,0:T(8,128)(2,1)} %bitcast.22), slice={[0:584], [384:512]} | slice | bytes 299008 | tf_op jit(solution)/shard_map/slice | solution.py:314
  4.1 0.1 collective-permute-start.1
  4.2 1.2 %copy.15 = bf16[73,8,512]{2,0,1:T(8,128)(2,1)S(1)} copy(bf16[73,8,512]{2,1,0:T(8,128)(2,1)} %param.7) | data formatting | bytes 1196032 | tf_op args[0]
  5.5 5.4 %shard_map.73 = (bf16[8,512,384]{2,1,0:T(8,128)(2,1)S(1)}, bf16[4,256,640]{2,1,0:T(8,128)(2,1)}, bf16[73,384]{1,0:T(8,128)(2,1)S(1)}, f32[1,384]{1,0:T(1,128)S(1...) custom-call(bf16[8,73,512]{2,1,0:T(8,128)(2,1)S(1)} %bitcast.18, bf16[73,384]{1,0:T(8,128)(2,1)} %w1_hbm.1, ...), custom_call_target="tpu_custom_call" | custom-call | flops 1437597696 | bytes 1048576 | tf_op jit(solution)/shard_map/pallas_call | solution.py:163
  10.8 1.9 %collective-permute-done = bf16[584,384]{1,0:T(8,128)(2,1)S(1)} collective-permute-done((bf16[584,384]{1,0:T(8,128)(2,1)S(1)}, bf16[584,384]{1,0:T(8,128)(2,1)S(1)}, u32[]{:S(2)}, u32[]{:S(2)}) %collective-permute-start) | collective-permute-done | bytes 448544 | tf_op jit(solution)/shard_map/ppermute | solution.py:314
  12.7 0.1 copy.16
  12.8 0.0 copy-start.1
  12.8 3.5 %shard_map.74.first_ref = bf16[2,8,384,384]{3,2,1,0:T(8,128)(2,1)S(1)} custom-call(bf16[8,73,384]{2,1,0:T(8,128)(2,1)S(1)} %bitcast.17, bf16[73,384]{1,0:T(8,128)(2,1)S(1)} %get-tuple-element.16.w1_ref, f32[1,384]{1,0:T(1,128)S(1)} %get-tuple-element.17.b1_ref, bf16[384,384]{1,0:T(8,128)(2,1)S(1)} %get-tuple-element.18.w2_ref, ...), custom_call_target="tpu_custom_call" | custom-call | flops 1078198272 | bytes 1048576 | tf_op jit(solution)/shard_map/pallas_call | solution.py:150
  16.3 0.0 collective-permute-done.1
  16.4 0.0 copy-done.1
  16.4 6.6 %shard_map.75 = bf16[16,2,2,8,3072]{4,3,2,1,0:T(8,128)(2,1)} custom-call(bf16[8,73,128]{2,1,0:T(8,128)(2,1)S(1)} %bitcast.19, bf16[73,384]{1,0:T(8,128)(2,1)S(1)} %get-tuple-element.16.w1_ref, f32[1,384]{1,0:T(1,128)S(1)} %get-tuple-element.17.b1_ref, bf16[384,384]{1,0:T(8,128)(2,1)S(1)} %get-tuple-element.18.w2_ref, f32[1,384]{1,0:T(1,128)S(1)} %get-tuple-element.19.b2_ref, ...), custom_call_target="tpu_custom_call" | custom-call | flops 3825205248 | bytes 4194304 | tf_op jit(solution)/shard_map/pallas_call | solution.py:241
  23.0 0.0 copy-start
  23.0 14.1 %all-to-all-start = ((bf16[64,8,3072]{2,1,0:T(8,128)(2,1)}), bf16[64,8,3072]{2,1,0:T(8,128)(2,1)}, u32[]{:S(2)}, u32[]{:S(2)}) async-start(bf16[64,8,3072]{2,1,0:T(8,128)(2,1)} %bitcast.20), calls=%async_computation | async-start | bytes 6291456 | tf_op jit(solution)/shard_map/all_to_all | solution.py:326
  37.1 0.1 collective-permute-start.2
  37.2 30.1 %collective-permute-done.2.packed_ref = bf16[4,256,640]{2,1,0:T(8,128)(2,1)S(1)} collective-permute-done((bf16[4,256,640]{2,1,0:T(8,128)(2,1)}, bf16[4,256,640]{2,1,0:T(8,128)(2,1)S(1)}, u32[]{:S(2)}, u32[]{:S(2)}) %collective-permute-start.2) | collective-permute-done | bytes 1310752 | tf_op jit(solution)/shard_map/ppermute | solution.py:324
  67.3 11.6 %all-to-all-done = bf16[64,8,3072]{2,1,0:T(8,128)(2,1)} async-done(((bf16[64,8,3072]{2,1,0:T(8,128)(2,1)}), bf16[64,8,3072]{2,1,0:T(8,128)(2,1)}, u32[]{:S(2)}, u32[]{:S(2)}) %all-to-all-start) | async-done | bytes 3145760 | tf_op jit(solution)/shard_map/all_to_all | solution.py:326
  78.9 0.0 copy-done
  78.9 5.5 %shard_map.76 = bf16[4,2,384,512]{3,2,1,0:T(8,128)(2,1)} custom-call(bf16[512,3072]{1,0:T(8,128)(2,1)} %bitcast.7.even_ref.odd_ref, bf16[512,3072]{1,0:T(8,128)(2,1)} %bitcast.7.even_ref.odd_ref, bf16[4,2,256,512]{3,2,1,0:T(8,128)(2,1)S(1)} %copy-done, bf16[4,256,640]{2,1,0:T(8,128)(2,1)S(1)} %collective-permute-done.2.packed_ref), custom_call_target="tpu_custom_call" | custom-call | flops 1610612736 | bytes 12582912 | tf_op jit(solution)/shard_map/pallas_call | solution.py:290
  (1 shorter events, 0.0 us)
Async XLA Ops:
  1.1 11.6 %collective-permute-start = (bf16[584,384]{1,0:T(8,128)(2,1)S(1)}, bf16[584,384]{1,0:T(8,128)(2,1)S(1)}, u32[]{:S(2)}, u32[]{:S(2)}) collective-permute-start(bf16[584,384]{1,0:T(8,128)(2,1)S(1)} %slice.8), channel_id=1, source_target_pairs={{0,1},{1,0},{2,3},{3,2},{4,5},{5,4},{6,7},{7,6},{8,9},{9,8},{10,11... | collective-permute-start | bytes 1345544 | tf_op jit(solution)/shard_map/ppermute | solution.py:314
  4.1 12.2 %collective-permute-start.1 = (bf16[584,128]{1,0:T(8,128)(2,1)S(1)}, bf16[584,128]{1,0:T(8,128)(2,1)S(1)}, u32[]{:S(2)}, u32[]{:S(2)}) collective-permute-start(bf16[584,128]{1,0:T(8,128)(2,1)S(1)} %slice.9), channel_id=1, source_target_pairs={{0,1},{1,0},{2,3},{3,2},{4,5},{5,4},{6,7},{7,6},{8,9},{9,8},{10,11... | collective-permute-start | bytes 448520 | tf_op jit(solution)/shard_map/ppermute | solution.py:314
  12.8 3.6 %copy-start.1 = (bf16[2,512,512]{2,1,0:T(8,128)(2,1)S(1)}, bf16[2,512,512]{2,1,0:T(8,128)(2,1)}, u32[]{:S(2)}) copy-start(bf16[2,512,512]{2,1,0:T(8,128)(2,1)} %constant.5.table_ref) | copy-start | bytes 3145732
  23.0 56.0 %copy-start = (bf16[4,2,256,512]{3,2,1,0:T(8,128)(2,1)S(1)}, bf16[4,2,256,512]{3,2,1,0:T(8,128)(2,1)}, u32[]{:S(2)}) copy-start(bf16[4,2,256,512]{3,2,1,0:T(8,128)(2,1)} %own_ref.1) | copy-start | bytes 6291460
  23.0 56.0 %all-to-all-start = ((bf16[64,8,3072]{2,1,0:T(8,128)(2,1)}), bf16[64,8,3072]{2,1,0:T(8,128)(2,1)}, u32[]{:S(2)}, u32[]{:S(2)}) async-start(bf16[64,8,3072]{2,1,0:T(8,128)(2,1)} %bitcast.20), calls=%async_computation | async-start | bytes 6291456 | tf_op jit(solution)/shard_map/all_to_all | solution.py:326
  37.1 30.2 %collective-permute-start.2 = (bf16[4,256,640]{2,1,0:T(8,128)(2,1)}, bf16[4,256,640]{2,1,0:T(8,128)(2,1)S(1)}, u32[]{:S(2)}, u32[]{:S(2)}) collective-permute-start(bf16[4,256,640]{2,1,0:T(8,128)(2,1)} %get-tuple-element.24), channel_id=1, source_target_pairs={{0,1},{1,0},{2,3},{3,2},{4,5},{5,4},{6,7},{7,6},{8,9},{9,8},{10,11... | collective-permute-start | bytes 3932168 | tf_op jit(solution)/shard_map/ppermute | solution.py:324

commit v3 on v2

--- a/solution.py
+++ b/solution.py
@@ -16,6 +16,7 @@
 LATS = 8
 CHUNK = 384
 LANE = 128
+OWN_TOGETHER, FIRST_TOGETHER, REST_TOGETHER = 2, 2, 8
 TILES = MM // LANE
 KEPT = (TILES + 1) * LANE
 ALL = ("lat", "lon")
@@ -28,8 +29,11 @@
     return (lat // 2) % 2
 
 
+LISTED = [2 * (OWNERS // 2 - 1 - at // 2) + at % 2 for at in range(OWNERS)]
+
+
 def groups():
-    return [[2 * lat + (owner_bit(lat) ^ group) for lat in range(OWNERS)] for group in range(2)]
+    return [[2 * lat + (owner_bit(lat) ^ group) for lat in LISTED] for group in range(2)]
 
 
 def my_group():
@@ -42,7 +46,7 @@
     for parity in range(2):
         rows = []
         for bit in range(2):
-            owner = np.array([lat for lat in range(OWNERS) if owner_bit(lat) == bit])
+            owner = np.array([lat for lat in LISTED if owner_bit(lat) == bit])
             for pair in range(PAIRS):
                 index = PAIRS * owner + pair
                 order = index if (pair + parity) % 2 == 0 else MM - 1 - index
@@ -110,7 +114,8 @@
     b1_ref[...] = b1_raw[...][None, :]
     w2_ref[...] = channel_order(w2_raw[...])
     b2_ref[...] = channel_order(b2_raw[...][None, :])
-    encode_kernel(x_ref, w1_ref, b1_ref, w2_ref, b2_ref, features_ref)
+    for lat, features in encode_lats(x_ref, w1_ref, b1_ref, w2_ref, b2_ref, OWN_TOGETHER):
+        features_ref[lat] = features
     result = pltpu.make_async_copy(staged, packed_ref, sent)
     for copy in copies:
         copy.wait()
@@ -118,9 +123,13 @@
     result.wait()
 
 
-def encode_kernel(x_ref, w1_ref, b1_ref, w2_ref, b2_ref, features_ref):
-    for lat in range(LATS):
-        features_ref[lat] = encode_rows(x_ref[lat], w1_ref[...], b1_ref[...], w2_ref[...], b2_ref[...])
+def encode_lats(x_ref, w1_ref, b1_ref, w2_ref, b2_ref, together):
+    lons = x_ref.shape[1] // LATS
+    for lat in range(0, LATS, together):
+        features = encode_rows(
+            x_ref[:, lat * lons:(lat + together) * lons], w1_ref[...], b1_ref[...], w2_ref[...], b2_ref[...])
+        for at in range(together):
+            yield lat + at, features[at * lons:(at + 1) * lons]
 
 
 IN_VMEM = pl.BlockSpec(memory_space=pltpu.VMEM)
@@ -139,14 +148,13 @@
 
 
 def first_kernel(x_ref, w1_ref, b1_ref, w2_ref, b2_ref, own_ref, parts_ref):
-    lons = x_ref.shape[2]
-    for lat in range(LATS):
-        theirs = encode_rows(x_ref[lat], w1_ref[...], b1_ref[...], w2_ref[...], b2_ref[...])
+    lons = x_ref.shape[1] // LATS
+    for lat, theirs in encode_lats(x_ref, w1_ref, b1_ref, w2_ref, b2_ref, FIRST_TOGETHER):
         parts_ref[0, lat], parts_ref[1, lat] = combine(own_ref[lat, :lons], theirs)
 
 
 def first_lons(x, encoder, own):
-    lats, _, lons = x.shape
+    lats, lons = LATS, x.shape[1] // LATS
     return pl.pallas_call(
         first_kernel,
         in_specs=[IN_VMEM] * 6,
@@ -158,7 +166,7 @@
 
 
 def encode_own(x, w1, b1, w2, b2, legendre):
-    lats, _, lons = x.shape
+    lats, lons = LATS, x.shape[1] // LATS
     pairs, _, rows, _ = legendre.shape
     return pl.pallas_call(
         encode_own_kernel,
@@ -188,25 +196,27 @@
 
 def transform_kernel(x_ref, w1_ref, b1_ref, w2_ref, b2_ref, own_ref, first_ref, table_ref, out_ref,
                      rest, held, staged, sems):
-    lons = x_ref.shape[2]
-    for lat in range(LATS):
-        theirs = encode_rows(x_ref[lat], w1_ref[...], b1_ref[...], w2_ref[...], b2_ref[...])
+    lons = x_ref.shape[1] // LATS
+    for lat, theirs in encode_lats(x_ref, w1_ref, b1_ref, w2_ref, b2_ref, REST_TOGETHER):
         rest[0, lat], rest[1, lat] = combine(own_ref[lat, HALF - lons:], theirs)
     copies = []
     for block in range(4):
         parity, bit = block // 2, block % 2
-        spectra_block(parity, bit, table_ref, (first_ref, rest), held.at[block], staged.at[block])
-        copies.append(pltpu.make_async_copy(
-            staged.at[block],
-            out_ref.at[:, bit, :, :, parity * PAIRS * C:(parity + 1) * PAIRS * C],
-            sems.at[block],
-        ))
-        copies[-1].start()
+        spectra_block(parity, bit, table_ref, (first_ref, rest), held.at[block])
+        for pair in range(PAIRS):
+            arrange(bit, held.at[block, pair], staged.at[block, pair])
+            slot = parity * PAIRS + pair
+            copies.append(pltpu.make_async_copy(
+                staged.at[block, pair],
+                out_ref.at[:, 1 - bit, :, :, slot * C:(slot + 1) * C],
+                sems.at[block, pair],
+            ))
+            copies[-1].start()
     for copy in copies:
         copy.wait()
 
 
-def spectra_block(parity, bit, table_ref, parts, held, staged):
+def spectra_block(parity, bit, table_ref, parts, held):
     owners = OWNERS // 2
     left = table_ref[parity, bit * 2 * PAIRS * owners:(bit + 1) * 2 * PAIRS * owners, :]
     for lat in range(LATS):
@@ -221,20 +231,17 @@
                 start = (pair * 2 + angle) * owners
                 for at in range(2):
                     held[pair, angle, at, rows, :] = result[start:start + owners, at * LANE:(at + 1) * LANE]
-    lane = lax.broadcasted_iota(jnp.int32, (owners * LATS, LANE), 1)
-    for pair in range(PAIRS):
-        real = held[pair, 0, 1]
-        imag = held[pair, 1, 1]
-        if bit == 0:
-            imag = pltpu.roll(imag, 64, 1)
-        else:
-            real = pltpu.roll(real, 64, 1)
-        pieces = (held[pair, 0, 0], held[pair, 1, 0], jnp.where(lane < 64, real, imag))
-        for at, piece in enumerate(pieces):
-            start = (pair * 3 + at) * LANE
-            staged[:, :, :, start:start + LANE] = (
-                piece.reshape(owners // 2, 2, LATS, LANE).astype(jnp.bfloat16)
-            )
+
+
+def arrange(bit, held, staged):
+    real, imag = held[0, 1], held[1, 1]
+    if bit == 0:
+        imag = pltpu.roll(imag, 64, 1)
+    else:
+        real = pltpu.roll(real, 64, 1)
+    lane = lax.broadcasted_iota(jnp.int32, real.shape, 1)
+    for at, piece in enumerate((held[0, 0], held[1, 0], jnp.where(lane < 64, real, imag))):
+        staged[:, :, :, at * LANE:(at + 1) * LANE] = piece.reshape(-1, 2, LATS, LANE).astype(jnp.bfloat16)
 
 
 def transform(x, encoder, own, first, table):
@@ -244,10 +251,10 @@
         out_specs=IN_HBM,
         out_shape=pltpu.HBM((OWNERS // 4, 2, 2, LATS, 2 * PAIRS * C), jnp.bfloat16),
         scratch_shapes=[
-            pltpu.VMEM((2, LATS, x.shape[2], C), jnp.bfloat16),
+            pltpu.VMEM((2, LATS, x.shape[1] // LATS, C), jnp.bfloat16),
             pltpu.VMEM((4, PAIRS, 2, 2, OWNERS // 2 * LATS, LANE), jnp.float32),
-            pltpu.VMEM((4, OWNERS // 4, 2, LATS, PAIRS * C), jnp.bfloat16),
-            pltpu.SemaphoreType.DMA((4,)),
+            pltpu.VMEM((4, PAIRS, OWNERS // 4, 2, LATS, C), jnp.bfloat16),
+            pltpu.SemaphoreType.DMA((4, PAIRS)),
         ],
         compiler_params=pltpu.CompilerParams(vmem_limit_bytes=MEDIUM),
         cost_estimate=pl.CostEstimate(flops=2 * LATS * HALF * C * (C // 2 + 2 * MM), bytes_accessed=4 * MIB,
@@ -255,67 +262,94 @@
     )(x, *encoder, own, first, table)
 
 
-def contract_kernel(even_ref, odd_ref, own_ref, packed_ref, out_ref, other):
+def contract_kernel(spectra_ref, own_ref, packed_ref, out_ref, other, spectra, staged, read, written):
     half = own_ref.shape[2]
+    reads = []
+    for slot in range(2 * PAIRS):
+        lanes = slice(slot * C, (slot + 1) * C)
+        reads.append(pltpu.make_async_copy(spectra_ref.at[:, lanes], spectra.at[:, lanes], read.at[slot]))
+    for pair in range(PAIRS):
+        reads[pair].start()
+        reads[PAIRS + pair].start()
     side = lax.axis_index("lon")
     block = order_block()
-    pair = pl.program_id(0)
-    index = lax.axis_index("lat") * PAIRS + pair
-    mine = pl.ds(pl.multiple_of(side * half, half), half)
-    theirs = pl.ds(pl.multiple_of((1 - side) * half, half), half)
     for tile in range(TILES + 1):
         member, place = tile_place(tile, block)
         lanes = pl.ds(pl.multiple_of(place * LANE, LANE), LANE)
-        other[member, :, lanes] = packed_ref[0, :, tile * LANE:(tile + 1) * LANE]
-    degree = lax.broadcasted_iota(jnp.int32, (C, MM), 1)
-    dims = (((0,), (0,)), ((), ()))
-    for parity, spectra_ref in enumerate((even_ref, odd_ref)):
-        member = (pair + parity) % 2
-        order = jnp.where(member == 0, index, MM - 1 - index)
-        values = lax.dot_general(
-            spectra_ref[mine, :], own_ref[0, member], dims, preferred_element_type=jnp.float32)
-        values += lax.dot_general(
-            spectra_ref[theirs, :], other[member], dims, preferred_element_type=jnp.float32)
-        values = jnp.where(degree >= order, values, 0.0).astype(jnp.bfloat16)
-        out_ref[0, member, 0:128] = values[0:128]
-        out_ref[0, member, 192:320] = values[128:256]
-        out_ref[0, member, 128:192] = values[256:320]
-        out_ref[0, member, 320:384] = values[320:384]
+        for pair in range(PAIRS):
+            other[pair, member, :, lanes] = packed_ref[pair, :, tile * LANE:(tile + 1) * LANE]
+
+    def products(full):
+        writes = []
+        for pair in range(PAIRS):
+            index = lax.axis_index("lat") * PAIRS + pair
+            reads[pair].wait()
+            reads[PAIRS + pair].wait()
+            for member in range(2):
+                slot = (pair + member) % 2 * PAIRS + pair
+                start = 0 if member == full else MM // 2
+                order = MM - 1 - index if member else index
+                values = 0.0
+                for which, held in ((side, own_ref), (1 - side, other)):
+                    values += lax.dot_general(
+                        by_latitude(spectra, which, half, slot), held[pair, member, :, start:],
+                        (((0,), (0,)), ((), ())), preferred_element_type=jnp.float32)
+                degree = lax.broadcasted_iota(jnp.int32, values.shape, 1) + start
+                values = jnp.where(degree >= order, values, 0.0).astype(jnp.bfloat16)
+                for at, to, count in ((0, 0, 128), (128, 192, 128), (256, 128, 64), (320, 320, 64)):
+                    staged[slot, to:to + count, start:] = values[at:at + count]
+                if start:
+                    staged[slot, :, :start] = jnp.zeros((C, start), jnp.bfloat16)
+                writes.append(pltpu.make_async_copy(staged.at[slot], out_ref.at[pair, member], written.at[slot]))
+                writes[-1].start()
+        for write in writes:
+            write.wait()
+
+    for full in range(2):
+        pl.when((block < TILES // 2) == (full == 0))(lambda full=full: products(full))
+
+
+def by_latitude(spectra, which, half, slot):
+    last = (1 - which) * half + half - 16
+    return jnp.concatenate([
+        spectra[pl.ds(pl.multiple_of(last - at, 16), 16), slot * C:(slot + 1) * C] for at in range(0, half, 16)
+    ], axis=0)
 
 
 def contract(spectra, legendre, packed):
-    rows = spectra.shape[0]
     half = legendre.shape[2]
     spectra = pltpu.with_memory_space_constraint(spectra, pltpu.HBM)
     return pl.pallas_call(
         contract_kernel,
-        grid=(PAIRS,),
-        in_specs=[
-            pl.BlockSpec((rows, C), lambda i: (0, i)),
-            pl.BlockSpec((rows, C), lambda i: (0, PAIRS + i)),
-            pl.BlockSpec((1, 2, half, MM), lambda i: (i, 0, 0, 0)),
-            pl.BlockSpec((1, half, KEPT), lambda i: (i, 0, 0)),
+        in_specs=[IN_HBM, IN_VMEM, IN_VMEM],
+        out_specs=IN_HBM,
+        out_shape=pltpu.HBM((PAIRS, 2, C, MM), jnp.bfloat16),
+        scratch_shapes=[
+            pltpu.VMEM((PAIRS, 2, half, MM), jnp.bfloat16),
+            pltpu.VMEM(spectra.shape, jnp.bfloat16),
+            pltpu.VMEM((2 * PAIRS, C, MM), jnp.bfloat16),
+            pltpu.SemaphoreType.DMA((2 * PAIRS,)),
+            pltpu.SemaphoreType.DMA((2 * PAIRS,)),
         ],
-        out_specs=pl.BlockSpec((1, 2, C, MM), lambda i: (i, 0, 0, 0)),
-        out_shape=jax.ShapeDtypeStruct((PAIRS, 2, C, MM), jnp.bfloat16),
-        scratch_shapes=[pltpu.VMEM((2, half, MM), jnp.bfloat16)],
-        compiler_params=pltpu.CompilerParams(vmem_limit_bytes=SMALL),
-        cost_estimate=pl.CostEstimate(flops=4 * PAIRS * rows * C * MM, bytes_accessed=12 * MIB, transcendentals=0),
-    )(spectra, spectra, legendre, packed)
+        compiler_params=pltpu.CompilerParams(vmem_limit_bytes=MEDIUM),
+        cost_estimate=pl.CostEstimate(flops=8 * PAIRS * half * C * MM, bytes_accessed=8 * MIB, transcendentals=0),
+    )(spectra, legendre, packed)
 
 
 def by_lat(flat):
-    return flat.reshape(-1, LATS, flat.shape[1]).transpose(1, 0, 2)
+    return flat.reshape(-1, LATS * flat.shape[1])
 
 
 def shards(state, in_weight, in_bias, out_weight, out_bias, legendre):
     swap = [(0, 1), (1, 0)]
     flat = state.reshape(-1, HALF)
-    received = [lax.ppermute(lons, "lon", swap) for lons in (flat[:, :CHUNK], flat[:, CHUNK:])]
+    received = [lax.ppermute(flat[:, :CHUNK], "lon", swap)]
     own, packed, *encoder = encode_own(
         by_lat(flat), *(
             pltpu.with_memory_space_constraint(array, pltpu.HBM)
             for array in (in_weight, in_bias, out_weight, out_bias, legendre)))
+    rest, own = lax.optimization_barrier((flat[:, CHUNK:], own))
+    received.append(lax.ppermute(rest, "lon", swap))
     first = first_lons(by_lat(received[0]), encoder, own)
     first, last = lax.optimization_barrier((first, received[1]))
     table = jnp.asarray(dft_tables()).astype(jnp.bfloat16)

time: 84.8 us -> 92.6 us (1.092)
  the two profiles are of different devices: /device:TPU:1 before, /device:TPU:9 now
where the time goes in v3:
time: 92.6 us; the launch traced here: 92 us
  waiting for transfers between devices  40.3 us (44%)
  Pallas kernels  19.3 us (21%)
  starting transfers between devices  16.9 us (18%)
  local copies, waits for them, and re-layouts  15.3 us (17%)
    ppermute x1, waiting for transfers between devices, shards(): packed = lax.ppermute(packed, 'lon', swap)  30.3 us
    all_to_all x1, starting transfers between devices, shards(): lax.all_to_all(spectra, ALL, split_axis=0, concat_axis=0, tiled=True, axi...  15.2 us
    unnamed x14, local copies, waits for them, and re-layouts  8.98 us
    all_to_all x1, waiting for transfers between devices, shards(): lax.all_to_all(spectra, ALL, split_axis=0, concat_axis=0, tiled=True, axi...  8.53 us
    pallas_call x1, Pallas kernels, transform(): pl.pallas_call(transform_kernel, in_specs=[IN_VMEM] * 8, out_specs=IN_HBM...  6.23 us
    pallas_call x1, Pallas kernels, encode_own(): pl.pallas_call(encode_own_kernel, in_specs=[IN_VMEM] + [IN_HBM] * 5, out_...  5.37 us
    pallas_call x1, Pallas kernels, contract(): pl.pallas_call(contract_kernel, in_specs=[IN_HBM, IN_VMEM, IN_VMEM], out_...  4.58 us
    reshape x2, local copies, waits for them, and re-layouts, by_lat(): return flat.reshape(-1, LATS * flat.shape[1])  3.66 us
  transfers between devices with their start and end apart: 4, of which 3 were waited for; matrix products, arithmetic and copies ran while one was open for 5% of the time, Pallas kernels for 9%

profile of v3, /device:TPU:9, one launch (start us, length us, event | category | flops | bytes accessed | tf_op | source)
XLA Modules:
  0.0 92.0 jit_solution(17335059098469177737)
XLA Ops:
  0.0 1.1 %slice.8 = bf16[584,384]{1,0:T(8,128)(2,1)S(1)} slice(bf16[584,512]{1,0:T(8,128)(2,1)} %bitcast.12), slice={[0:584], [0:384]} | slice | bytes 897024 | tf_op jit(solution)/shard_map/slice | solution.py:346
  1.1 1.3 %collective-permute-start = (bf16[584,384]{1,0:T(8,128)(2,1)S(1)}, bf16[584,384]{1,0:T(8,128)(2,1)}, u32[]{:S(2)}, u32[]{:S(2)}) collective-permute-start(bf16[584,384]{1,0:T(8,128)(2,1)S(1)} %slice.8), channel_id=1, source_target_pairs={{0,1},{1,0},{2,3},{3,2},{4,5},{5,4},{6,7},{7,6},{8,9},{9,8},{10,11... | collective-permute-start | bytes 1345544 | tf_op jit(solution)/shard_map/ppermute | solution.py:346
  2.4 1.6 %slice.9 = bf16[584,128]{1,0:T(8,128)(2,1)} slice(bf16[584,512]{1,0:T(8,128)(2,1)} %bitcast.13), slice={[0:584], [384:512]} | slice | bytes 299008 | tf_op jit(solution)/shard_map/slice | solution.py:351
  3.9 1.1 %pad = bf16[80,8,512]{2,1,0:T(8,128)(2,1)S(1)} pad(bf16[73,8,512]{2,1,0:T(8,128)(2,1)} %param.7, bf16[]{:T(256)} %constant.6), padding=0_7x0_0x0_0 | pad | bytes 1253378
  5.0 0.2 copy.8
  5.3 5.4 %shard_map.73 = (bf16[8,512,384]{2,1,0:T(8,128)(2,1)S(1)}, bf16[4,256,640]{2,1,0:T(8,128)(2,1)}, bf16[73,384]{1,0:T(8,128)(2,1)S(1)}, f32[1,384]{1,0:T(1,128)S(1...) custom-call(bf16[73,4096]{1,0:T(8,128)(2,1)S(1)} %bitcast.9, bf16[73,384]{1,0:T(8,128)(2,1)} %w1_hbm.1, f32[384]{0:T(512)} %b1_hbm.1, ...), custom_call_target="tpu_custom_call" | custom-call | flops 1437597696 | bytes 1048576 | tf_op jit(solution)/shard_map/pallas_call | solution.py:171
  10.6 0.3 collective-permute-start.1
  11.0 1.4 %collective-permute-done = bf16[584,384]{1,0:T(8,128)(2,1)} collective-permute-done((bf16[584,384]{1,0:T(8,128)(2,1)S(1)}, bf16[584,384]{1,0:T(8,128)(2,1)}, u32[]{:S(2)}, u32[]{:S(2)}) %collective-permute-start) | collective-permute-done | bytes 448544 | tf_op jit(solution)/shard_map/ppermute | solution.py:346
  12.4 2.0 %reshape.19.x_ref = bf16[73,3072]{1,0:T(8,128)(2,1)} reshape(bf16[584,384]{1,0:T(8,128)(2,1)} %collective-permute-done) | data formatting | bytes 897024 | tf_op jit(solution)/shard_map/reshape | solution.py:340
  14.4 0.0 copy-start.3
  14.4 1.0 %copy-done.3 = bf16[73,3072]{1,0:T(8,128)(2,1)S(1)} copy-done((bf16[73,3072]{1,0:T(8,128)(2,1)S(1)}, bf16[73,3072]{1,0:T(8,128)(2,1)}, u32[]{:S(2)}) %copy-start.3) | copy-done | bytes 448536
  15.5 3.1 %shard_map.74.first_ref = bf16[2,8,384,384]{3,2,1,0:T(8,128)(2,1)S(1)} custom-call(bf16[73,3072]{1,0:T(8,128)(2,1)S(1)} %copy-done.3, bf16[73,384]{1,0:T(8,128)(2,1)S(1)} %get-tuple-element.18.w1_ref, f32[1,384]{1,0:T(1,128)S(1)} %get-tuple-element.19.b1_ref, bf16[384,384]{1,0:T(8,128)(2,1)S(1)} %get-tuple-element.20.w2_ref, ...), custom_call_target="tpu_custom_call" | custom-call | flops 1078198272 | bytes 1048576 | tf_op jit(solution)/shard_map/pallas_call | solution.py:158
  18.6 0.0 copy-start
  18.6 2.1 %copy-done = bf16[2,8,384,384]{3,2,1,0:T(8,128)(2,1)} copy-done((bf16[2,8,384,384]{3,2,1,0:T(8,128)(2,1)}, bf16[2,8,384,384]{3,2,1,0:T(8,128)(2,1)S(1)}, u32[]{:S(2)}) %copy-start) | copy-done | bytes 4718616
  20.7 0.0 collective-permute-done.1
  20.7 1.6 %reshape.20.x_ref = bf16[73,1024]{1,0:T(8,128)(2,1)} reshape(bf16[584,128]{1,0:T(8,128)(2,1)} %collective-permute-done.1) | data formatting | bytes 299008 | tf_op jit(solution)/shard_map/reshape | solution.py:340
  22.4 0.0 copy-start.1
  22.4 2.3 %copy-done.1 = bf16[2,8,384,384]{3,2,1,0:T(8,128)(2,1)S(1)} copy-done((bf16[2,8,384,384]{3,2,1,0:T(8,128)(2,1)S(1)}, bf16[2,8,384,384]{3,2,1,0:T(8,128)(2,1)}, u32[]{:S(2)}) %copy-start.1) | copy-done | bytes 4718616
  24.7 0.0 copy-start.4
  24.7 0.9 copy-done.4
  25.6 0.0 copy-start.5
  25.6 1.2 %copy-done.5 = bf16[2,512,512]{2,1,0:T(8,128)(2,1)S(1)} copy-done((bf16[2,512,512]{2,1,0:T(8,128)(2,1)S(1)}, bf16[2,512,512]{2,1,0:T(8,128)(2,1)}, u32[]{:S(2)}) %copy-start.5) | copy-done | bytes 1048600
  26.9 6.2 %shard_map.75 = bf16[16,2,2,8,3072]{4,3,2,1,0:T(8,128)(2,1)} custom-call(bf16[73,1024]{1,0:T(8,128)(2,1)S(1)} %copy-done.4, bf16[73,384]{1,0:T(8,128)(2,1)S(1)} %get-tuple-element.18.w1_ref, f32[1,384]{1,0:T(1,128)S(1)} %get-tuple-element.19.b1_ref, bf16[384,384]{1,0:T(8,128)(2,1)S(1)} %get-tuple-element.20.w2_ref, f32[1,384]{1,0:T(1,128)S(1)} %get-tuple-element.21.b2_ref, ...), custom_call_target="tpu_custom_call" | custom-call | flops 3825205248 | bytes 4194304 | tf_op jit(solution)/shard_map/pallas_call | solution.py:248
  33.1 0.0 copy-start.2
  33.1 15.2 %all-to-all-start = ((bf16[64,8,3072]{2,1,0:T(8,128)(2,1)}), bf16[64,8,3072]{2,1,0:T(8,128)(2,1)}, u32[]{:S(2)}, u32[]{:S(2)}) async-start(bf16[64,8,3072]{2,1,0:T(8,128)(2,1)} %bitcast.10), calls=%async_computation | async-start | bytes 6291456 | tf_op jit(solution)/shard_map/all_to_all | solution.py:360
  48.3 0.1 collective-permute-start.2
  48.4 30.3 %collective-permute-done.2.packed_ref = bf16[4,256,640]{2,1,0:T(8,128)(2,1)S(1)} collective-permute-done((bf16[4,256,640]{2,1,0:T(8,128)(2,1)}, bf16[4,256,640]{2,1,0:T(8,128)(2,1)S(1)}, u32[]{:S(2)}, u32[]{:S(2)}) %collective-permute-start.2) | collective-permute-done | bytes 1310752 | tf_op jit(solution)/shard_map/ppermute | solution.py:358
  78.7 8.5 %all-to-all-done = bf16[64,8,3072]{2,1,0:T(8,128)(2,1)} async-done(((bf16[64,8,3072]{2,1,0:T(8,128)(2,1)}), bf16[64,8,3072]{2,1,0:T(8,128)(2,1)}, u32[]{:S(2)}, u32[]{:S(2)}) %all-to-all-start) | async-done | bytes 3145760 | tf_op jit(solution)/shard_map/all_to_all | solution.py:360
  87.3 0.0 copy-done.2
  87.3 4.6 %shard_map.76 = bf16[4,2,384,512]{3,2,1,0:T(8,128)(2,1)} custom-call(bf16[512,3072]{1,0:T(8,128)(2,1)} %bitcast.2.spectra_ref, bf16[4,2,256,512]{3,2,1,0:T(8,128)(2,1)S(1)} %copy-done.2, bf16[4,256,640]{2,1,0:T(8,128)(2,1)S(1)} %collective-permute-done.2.packed_ref), custom_call_target="tpu_custom_call" | custom-call | flops 1610612736 | bytes 8388608 | tf_op jit(solution)/shard_map/pallas_call | solution.py:322
Async XLA Ops:
  1.1 11.4 %collective-permute-start = (bf16[584,384]{1,0:T(8,128)(2,1)S(1)}, bf16[584,384]{1,0:T(8,128)(2,1)}, u32[]{:S(2)}, u32[]{:S(2)}) collective-permute-start(bf16[584,384]{1,0:T(8,128)(2,1)S(1)} %slice.8), channel_id=1, source_target_pairs={{0,1},{1,0},{2,3},{3,2},{4,5},{5,4},{6,7},{7,6},{8,9},{9,8},{10,11... | collective-permute-start | bytes 1345544 | tf_op jit(solution)/shard_map/ppermute | solution.py:346
  10.6 10.1 %collective-permute-start.1 = (bf16[584,128]{1,0:T(8,128)(2,1)}, bf16[584,128]{1,0:T(8,128)(2,1)}, u32[]{:S(2)}, u32[]{:S(2)}) collective-permute-start(bf16[584,128]{1,0:T(8,128)(2,1)} %slice.9), channel_id=1, source_target_pairs={{0,1},{1,0},{2,3},{3,2},{4,5},{5,4},{6,7},{7,6},{8,9},{9,8},{10,11... | collective-permute-start | bytes 448520 | tf_op jit(solution)/shard_map/ppermute | solution.py:352
  14.4 1.0 %copy-start.3 = (bf16[73,3072]{1,0:T(8,128)(2,1)S(1)}, bf16[73,3072]{1,0:T(8,128)(2,1)}, u32[]{:S(2)}) copy-start(bf16[73,3072]{1,0:T(8,128)(2,1)} %reshape.19.x_ref) | copy-start | bytes 1345540
  18.6 2.1 %copy-start = (bf16[2,8,384,384]{3,2,1,0:T(8,128)(2,1)}, bf16[2,8,384,384]{3,2,1,0:T(8,128)(2,1)S(1)}, u32[]{:S(2)}) copy-start(bf16[2,8,384,384]{3,2,1,0:T(8,128)(2,1)S(1)} %shard_map.74.first_ref) | copy-start | bytes 14155780
  22.4 2.3 %copy-start.1 = (bf16[2,8,384,384]{3,2,1,0:T(8,128)(2,1)S(1)}, bf16[2,8,384,384]{3,2,1,0:T(8,128)(2,1)}, u32[]{:S(2)}) copy-start(bf16[2,8,384,384]{3,2,1,0:T(8,128)(2,1)} %copy-done) | copy-start | bytes 14155780
  24.7 0.9 copy-start.4
  25.6 1.2 %copy-start.5 = (bf16[2,512,512]{2,1,0:T(8,128)(2,1)S(1)}, bf16[2,512,512]{2,1,0:T(8,128)(2,1)}, u32[]{:S(2)}) copy-start(bf16[2,512,512]{2,1,0:T(8,128)(2,1)} %constant.5.table_ref) | copy-start | bytes 3145732
  33.1 54.2 %copy-start.2 = (bf16[4,2,256,512]{3,2,1,0:T(8,128)(2,1)S(1)}, bf16[4,2,256,512]{3,2,1,0:T(8,128)(2,1)}, u32[]{:S(2)}) copy-start(bf16[4,2,256,512]{3,2,1,0:T(8,128)(2,1)} %own_ref.1) | copy-start | bytes 6291460
  33.1 54.2 %all-to-all-start = ((bf16[64,8,3072]{2,1,0:T(8,128)(2,1)}), bf16[64,8,3072]{2,1,0:T(8,128)(2,1)}, u32[]{:S(2)}, u32[]{:S(2)}) async-start(bf16[64,8,3072]{2,1,0:T(8,128)(2,1)} %bitcast.10), calls=%async_computation | async-start | bytes 6291456 | tf_op jit(solution)/shard_map/all_to_all | solution.py:360
  48.3 30.4 %collective-permute-start.2 = (bf16[4,256,640]{2,1,0:T(8,128)(2,1)}, bf16[4,256,640]{2,1,0:T(8,128)(2,1)S(1)}, u32[]{:S(2)}, u32[]{:S(2)}) collective-permute-start(bf16[4,256,640]{2,1,0:T(8,128)(2,1)} %get-tuple-element.28), channel_id=1, source_target_pairs={{0,1},{1,0},{2,3},{3,2},{4,5},{5,4},{6,7},{7,6},{8,9},{9,8},{10,11... | collective-permute-start | bytes 3932168 | tf_op jit(solution)/shard_map/ppermute | solution.py:358

commit v4 on v3

--- a/solution.py
+++ b/solution.py
@@ -29,7 +29,9 @@
     return (lat // 2) % 2
 
 
-LISTED = [2 * (OWNERS // 2 - 1 - at // 2) + at % 2 for at in range(OWNERS)]
+PLACES = [4 * z + y for y in range(3, -1, -1) for z in range(3, -1, -1)]
+BITS = (0, 1)
+LISTED = [4 * place + 2 * bit + core for place in PLACES for bit in BITS for core in range(2)]
 
 
 def groups():
@@ -124,10 +126,10 @@
 
 
 def encode_lats(x_ref, w1_ref, b1_ref, w2_ref, b2_ref, together):
-    lons = x_ref.shape[1] // LATS
+    lons = x_ref.shape[2]
     for lat in range(0, LATS, together):
-        features = encode_rows(
-            x_ref[:, lat * lons:(lat + together) * lons], w1_ref[...], b1_ref[...], w2_ref[...], b2_ref[...])
+        rows = jnp.concatenate([x_ref[lat + at] for at in range(together)], axis=1)
+        features = encode_rows(rows, w1_ref[...], b1_ref[...], w2_ref[...], b2_ref[...])
         for at in range(together):
             yield lat + at, features[at * lons:(at + 1) * lons]
 
@@ -148,13 +150,13 @@
 
 
 def first_kernel(x_ref, w1_ref, b1_ref, w2_ref, b2_ref, own_ref, parts_ref):
-    lons = x_ref.shape[1] // LATS
+    lons = x_ref.shape[2]
     for lat, theirs in encode_lats(x_ref, w1_ref, b1_ref, w2_ref, b2_ref, FIRST_TOGETHER):
         parts_ref[0, lat], parts_ref[1, lat] = combine(own_ref[lat, :lons], theirs)
 
 
 def first_lons(x, encoder, own):
-    lats, lons = LATS, x.shape[1] // LATS
+    lats, _, lons = x.shape
     return pl.pallas_call(
         first_kernel,
         in_specs=[IN_VMEM] * 6,
@@ -166,7 +168,7 @@
 
 
 def encode_own(x, w1, b1, w2, b2, legendre):
-    lats, lons = LATS, x.shape[1] // LATS
+    lats, _, lons = x.shape
     pairs, _, rows, _ = legendre.shape
     return pl.pallas_call(
         encode_own_kernel,
@@ -196,7 +198,7 @@
 
 def transform_kernel(x_ref, w1_ref, b1_ref, w2_ref, b2_ref, own_ref, first_ref, table_ref, out_ref,
                      rest, held, staged, sems):
-    lons = x_ref.shape[1] // LATS
+    lons = x_ref.shape[2]
     for lat, theirs in encode_lats(x_ref, w1_ref, b1_ref, w2_ref, b2_ref, REST_TOGETHER):
         rest[0, lat], rest[1, lat] = combine(own_ref[lat, HALF - lons:], theirs)
     copies = []
@@ -208,7 +210,7 @@
             slot = parity * PAIRS + pair
             copies.append(pltpu.make_async_copy(
                 staged.at[block, pair],
-                out_ref.at[:, 1 - bit, :, :, slot * C:(slot + 1) * C],
+                out_ref.at[:, BITS.index(bit), :, :, slot * C:(slot + 1) * C],
                 sems.at[block, pair],
             ))
             copies[-1].start()
@@ -251,7 +253,7 @@
         out_specs=IN_HBM,
         out_shape=pltpu.HBM((OWNERS // 4, 2, 2, LATS, 2 * PAIRS * C), jnp.bfloat16),
         scratch_shapes=[
-            pltpu.VMEM((2, LATS, x.shape[1] // LATS, C), jnp.bfloat16),
+            pltpu.VMEM((2, LATS, x.shape[2], C), jnp.bfloat16),
             pltpu.VMEM((4, PAIRS, 2, 2, OWNERS // 2 * LATS, LANE), jnp.float32),
             pltpu.VMEM((4, PAIRS, OWNERS // 4, 2, LATS, C), jnp.bfloat16),
             pltpu.SemaphoreType.DMA((4, PAIRS)),
@@ -310,10 +312,12 @@
 
 
 def by_latitude(spectra, which, half, slot):
-    last = (1 - which) * half + half - 16
-    return jnp.concatenate([
-        spectra[pl.ds(pl.multiple_of(last - at, 16), 16), slot * C:(slot + 1) * C] for at in range(0, half, 16)
-    ], axis=0)
+    pieces = []
+    for at in range(half // 16):
+        first, second = (LISTED.index(2 * index) // 2 for index in (at, at + half // 16))
+        start = pl.multiple_of(16 * jnp.where(which == 0, first, second), 16)
+        pieces.append(spectra[pl.ds(start, 16), slot * C:(slot + 1) * C])
+    return jnp.concatenate(pieces, axis=0)
 
 
 def contract(spectra, legendre, packed):
@@ -337,7 +341,7 @@
 
 
 def by_lat(flat):
-    return flat.reshape(-1, LATS * flat.shape[1])
+    return flat.reshape(-1, LATS, flat.shape[1]).transpose(1, 0, 2)
 
 
 def shards(state, in_weight, in_bias, out_weight, out_bias, legendre):

time: 92.6 us -> 79.9 us (0.86)
  the two profiles are of different devices: /device:TPU:9 before, /device:TPU:1 now
where the time goes in v4:
time: 79.9 us; the launch traced here: 79.5 us
  waiting for transfers between devices  38.7 us (48%)
  Pallas kernels  19.3 us (24%)
  starting transfers between devices  18 us (23%)
  local copies, waits for them, and re-layouts  3.33 us (4%)
    ppermute x1, waiting for transfers between devices, shards(): packed = lax.ppermute(packed, 'lon', swap)  29.3 us
    all_to_all x1, starting transfers between devices, shards(): lax.all_to_all(spectra, ALL, split_axis=0, concat_axis=0, tiled=True, axi...  14.7 us
    all_to_all x1, waiting for transfers between devices, shards(): lax.all_to_all(spectra, ALL, split_axis=0, concat_axis=0, tiled=True, axi...  7 us
    pallas_call x1, Pallas kernels, transform(): pl.pallas_call(transform_kernel, in_specs=[IN_VMEM] * 8, out_specs=IN_HBM...  6.29 us
    pallas_call x1, Pallas kernels, encode_own(): pl.pallas_call(encode_own_kernel, in_specs=[IN_VMEM] + [IN_HBM] * 5, out_...  5.32 us
    pallas_call x1, Pallas kernels, contract(): pl.pallas_call(contract_kernel, in_specs=[IN_HBM, IN_VMEM, IN_VMEM], out_...  4.6 us
    pallas_call x1, Pallas kernels, first_lons(): pl.pallas_call(first_kernel, in_specs=[IN_VMEM] * 6, out_specs=IN_VMEM, o...  3.06 us
    ppermute x1, starting transfers between devices, shards(): received = [lax.ppermute(flat[:, :CHUNK], 'lon', swap)]  2.12 us
  transfers between devices with their start and end apart: 4, of which 4 were waited for; matrix products, arithmetic and copies ran while one was open for 3% of the time, Pallas kernels for 11%

profile of v4, /device:TPU:1, one launch (start us, length us, event | category | flops | bytes accessed | tf_op | source)
XLA Modules:
  0.0 79.5 jit_solution(15745313485595516779)
XLA Ops:
  0.0 1.1 %slice.8 = bf16[584,384]{1,0:T(8,128)(2,1)S(1)} slice(bf16[584,512]{1,0:T(8,128)(2,1)} %bitcast.21), slice={[0:584], [0:384]} | slice | bytes 897024 | tf_op jit(solution)/shard_map/slice | solution.py:350
  1.1 2.1 %collective-permute-start = (bf16[584,384]{1,0:T(8,128)(2,1)S(1)}, bf16[584,384]{1,0:T(8,128)(2,1)S(1)}, u32[]{:S(2)}, u32[]{:S(2)}) collective-permute-start(bf16[584,384]{1,0:T(8,128)(2,1)S(1)} %slice.8), channel_id=1, source_target_pairs={{0,1},{1,0},{2,3},{3,2},{4,5},{5,4},{6,7},{7,6},{8,9},{9,8},{10,11... | collective-permute-start | bytes 1345544 | tf_op jit(solution)/shard_map/ppermute | solution.py:350
  3.2 0.9 %slice.9 = bf16[584,128]{1,0:T(8,128)(2,1)S(1)} slice(bf16[584,512]{1,0:T(8,128)(2,1)} %bitcast.22), slice={[0:584], [384:512]} | slice | bytes 299008 | tf_op jit(solution)/shard_map/slice | solution.py:355
  4.1 1.2 %copy.15 = bf16[73,8,512]{2,0,1:T(8,128)(2,1)S(1)} copy(bf16[73,8,512]{2,1,0:T(8,128)(2,1)} %param.7) | data formatting | bytes 1196032 | tf_op args[0]
  5.4 5.3 %shard_map.73 = (bf16[8,512,384]{2,1,0:T(8,128)(2,1)S(1)}, bf16[4,256,640]{2,1,0:T(8,128)(2,1)}, bf16[73,384]{1,0:T(8,128)(2,1)S(1)}, f32[1,384]{1,0:T(1,128)S(1...) custom-call(bf16[8,73,512]{2,1,0:T(8,128)(2,1)S(1)} %bitcast.18, bf16[73,384]{1,0:T(8,128)(2,1)} %w1_hbm.1, ...), custom_call_target="tpu_custom_call" | custom-call | flops 1437597696 | bytes 1048576 | tf_op jit(solution)/shard_map/pallas_call | solution.py:173
  10.7 0.1 collective-permute-start.1
  10.8 1.9 %collective-permute-done = bf16[584,384]{1,0:T(8,128)(2,1)S(1)} collective-permute-done((bf16[584,384]{1,0:T(8,128)(2,1)S(1)}, bf16[584,384]{1,0:T(8,128)(2,1)S(1)}, u32[]{:S(2)}, u32[]{:S(2)}) %collective-permute-start) | collective-permute-done | bytes 448544 | tf_op jit(solution)/shard_map/ppermute | solution.py:350
  12.7 0.1 copy.16
  12.8 0.0 copy-start.1
  12.8 3.1 %shard_map.74.first_ref = bf16[2,8,384,384]{3,2,1,0:T(8,128)(2,1)S(1)} custom-call(bf16[8,73,384]{2,1,0:T(8,128)(2,1)S(1)} %bitcast.17, bf16[73,384]{1,0:T(8,128)(2,1)S(1)} %get-tuple-element.18.w1_ref, f32[1,384]{1,0:T(1,128)S(1)} %get-tuple-element.19.b1_ref, bf16[384,384]{1,0:T(8,128)(2,1)S(1)} %get-tuple-element.20.w2_ref, ...), custom_call_target="tpu_custom_call" | custom-call | flops 1078198272 | bytes 1048576 | tf_op jit(solution)/shard_map/pallas_call | solution.py:160
  15.8 0.5 collective-permute-done.1
  16.4 0.0 copy-done.1
  16.4 6.3 %shard_map.75 = bf16[16,2,2,8,3072]{4,3,2,1,0:T(8,128)(2,1)} custom-call(bf16[8,73,128]{2,1,0:T(8,128)(2,1)S(1)} %bitcast.19, bf16[73,384]{1,0:T(8,128)(2,1)S(1)} %get-tuple-element.18.w1_ref, f32[1,384]{1,0:T(1,128)S(1)} %get-tuple-element.19.b1_ref, bf16[384,384]{1,0:T(8,128)(2,1)S(1)} %get-tuple-element.20.w2_ref, f32[1,384]{1,0:T(1,128)S(1)} %get-tuple-element.21.b2_ref, ...), custom_call_target="tpu_custom_call" | custom-call | flops 3825205248 | bytes 4194304 | tf_op jit(solution)/shard_map/pallas_call | solution.py:250
  22.7 0.0 copy-start
  22.7 14.7 %all-to-all-start = ((bf16[64,8,3072]{2,1,0:T(8,128)(2,1)}), bf16[64,8,3072]{2,1,0:T(8,128)(2,1)}, u32[]{:S(2)}, u32[]{:S(2)}) async-start(bf16[64,8,3072]{2,1,0:T(8,128)(2,1)} %bitcast.20), calls=%async_computation | async-start | bytes 6291456 | tf_op jit(solution)/shard_map/all_to_all | solution.py:364
  37.4 1.1 %collective-permute-start.2 = (bf16[4,256,640]{2,1,0:T(8,128)(2,1)}, bf16[4,256,640]{2,1,0:T(8,128)(2,1)S(1)}, u32[]{:S(2)}, u32[]{:S(2)}) collective-permute-start(bf16[4,256,640]{2,1,0:T(8,128)(2,1)} %get-tuple-element.28), channel_id=1, source_target_pairs={{0,1},{1,0},{2,3},{3,2},{4,5},{5,4},{6,7},{7,6},{8,9},{9,8},{10,11... | collective-permute-start | bytes 3932168 | tf_op jit(solution)/shard_map/ppermute | solution.py:362
  38.5 29.3 %collective-permute-done.2.packed_ref = bf16[4,256,640]{2,1,0:T(8,128)(2,1)S(1)} collective-permute-done((bf16[4,256,640]{2,1,0:T(8,128)(2,1)}, bf16[4,256,640]{2,1,0:T(8,128)(2,1)S(1)}, u32[]{:S(2)}, u32[]{:S(2)}) %collective-permute-start.2) | collective-permute-done | bytes 1310752 | tf_op jit(solution)/shard_map/ppermute | solution.py:362
  67.8 7.0 %all-to-all-done = bf16[64,8,3072]{2,1,0:T(8,128)(2,1)} async-done(((bf16[64,8,3072]{2,1,0:T(8,128)(2,1)}), bf16[64,8,3072]{2,1,0:T(8,128)(2,1)}, u32[]{:S(2)}, u32[]{:S(2)}) %all-to-all-start) | async-done | bytes 3145760 | tf_op jit(solution)/shard_map/all_to_all | solution.py:364
  74.8 0.0 copy-done
  74.8 4.6 %shard_map.76 = bf16[4,2,384,512]{3,2,1,0:T(8,128)(2,1)} custom-call(bf16[512,3072]{1,0:T(8,128)(2,1)} %bitcast.7.spectra_ref, bf16[4,2,256,512]{3,2,1,0:T(8,128)(2,1)S(1)} %copy-done, bf16[4,256,640]{2,1,0:T(8,128)(2,1)S(1)} %collective-permute-done.2.packed_ref), custom_call_target="tpu_custom_call" | custom-call | flops 1610612736 | bytes 8388608 | tf_op jit(solution)/shard_map/pallas_call | solution.py:326
  (1 shorter events, 0.0 us)
Async XLA Ops:
  1.1 11.6 %collective-permute-start = (bf16[584,384]{1,0:T(8,128)(2,1)S(1)}, bf16[584,384]{1,0:T(8,128)(2,1)S(1)}, u32[]{:S(2)}, u32[]{:S(2)}) collective-permute-start(bf16[584,384]{1,0:T(8,128)(2,1)S(1)} %slice.8), channel_id=1, source_target_pairs={{0,1},{1,0},{2,3},{3,2},{4,5},{5,4},{6,7},{7,6},{8,9},{9,8},{10,11... | collective-permute-start | bytes 1345544 | tf_op jit(solution)/shard_map/ppermute | solution.py:350
  10.7 5.7 %collective-permute-start.1 = (bf16[584,128]{1,0:T(8,128)(2,1)S(1)}, bf16[584,128]{1,0:T(8,128)(2,1)S(1)}, u32[]{:S(2)}, u32[]{:S(2)}) collective-permute-start(bf16[584,128]{1,0:T(8,128)(2,1)S(1)} %slice.9), channel_id=1, source_target_pairs={{0,1},{1,0},{2,3},{3,2},{4,5},{5,4},{6,7},{7,6},{8,9},{9,8},{10,11... | collective-permute-start | bytes 448520 | tf_op jit(solution)/shard_map/ppermute | solution.py:356
  12.8 3.6 %copy-start.1 = (bf16[2,512,512]{2,1,0:T(8,128)(2,1)S(1)}, bf16[2,512,512]{2,1,0:T(8,128)(2,1)}, u32[]{:S(2)}) copy-start(bf16[2,512,512]{2,1,0:T(8,128)(2,1)} %constant.5.table_ref) | copy-start | bytes 3145732
  22.7 52.1 %copy-start = (bf16[4,2,256,512]{3,2,1,0:T(8,128)(2,1)S(1)}, bf16[4,2,256,512]{3,2,1,0:T(8,128)(2,1)}, u32[]{:S(2)}) copy-start(bf16[4,2,256,512]{3,2,1,0:T(8,128)(2,1)} %own_ref.1) | copy-start | bytes 6291460
  22.7 52.1 %all-to-all-start = ((bf16[64,8,3072]{2,1,0:T(8,128)(2,1)}), bf16[64,8,3072]{2,1,0:T(8,128)(2,1)}, u32[]{:S(2)}, u32[]{:S(2)}) async-start(bf16[64,8,3072]{2,1,0:T(8,128)(2,1)} %bitcast.20), calls=%async_computation | async-start | bytes 6291456 | tf_op jit(solution)/shard_map/all_to_all | solution.py:364
  37.4 30.4 %collective-permute-start.2 = (bf16[4,256,640]{2,1,0:T(8,128)(2,1)}, bf16[4,256,640]{2,1,0:T(8,128)(2,1)S(1)}, u32[]{:S(2)}, u32[]{:S(2)}) collective-permute-start(bf16[4,256,640]{2,1,0:T(8,128)(2,1)} %get-tuple-element.28), channel_id=1, source_target_pairs={{0,1},{1,0},{2,3},{3,2},{4,5},{5,4},{6,7},{7,6},{8,9},{9,8},{10,11... | collective-permute-start | bytes 3932168 | tf_op jit(solution)/shard_map/ppermute | solution.py:362

commit v5 on v4

--- a/solution.py
+++ b/solution.py
@@ -16,9 +16,11 @@
 LATS = 8
 CHUNK = 384
 LANE = 128
+TOGETHER = 2
 OWN_TOGETHER, FIRST_TOGETHER, REST_TOGETHER = 2, 2, 8
 TILES = MM // LANE
 KEPT = (TILES + 1) * LANE
+SECOND_FROM = MM // 2
 ALL = ("lat", "lon")
 MIB = 1 << 20
 SMALL = 16 * MIB
@@ -264,7 +266,7 @@
     )(x, *encoder, own, first, table)
 
 
-def contract_kernel(spectra_ref, own_ref, packed_ref, out_ref, other, spectra, staged, read, written):
+def contract_kernel(spectra_ref, own_ref, packed_ref, out_ref, kept, spectra, staged, read, written):
     half = own_ref.shape[2]
     reads = []
     for slot in range(2 * PAIRS):
@@ -273,55 +275,56 @@
     for pair in range(PAIRS):
         reads[pair].start()
         reads[PAIRS + pair].start()
+    assemble(own_ref, packed_ref, kept, half)
+    writes = []
+    for pair in range(PAIRS):
+        index = lax.axis_index("lat") * PAIRS + pair
+        if pair % TOGETHER == 0:
+            for at in range(pair, pair + TOGETHER):
+                reads[at].wait()
+                reads[PAIRS + at].wait()
+        for member in range(2):
+            slot = (pair + member) % 2 * PAIRS + pair
+            start = member * SECOND_FROM
+            order = MM - 1 - index if member else index
+            values = lax.dot_general(
+                by_latitude(spectra, slot), kept[pair, member, :, start:],
+                (((0,), (0,)), ((), ())), preferred_element_type=jnp.float32)
+            degree = lax.broadcasted_iota(jnp.int32, values.shape, 1) + start
+            values = jnp.where(degree >= order, values, 0.0).astype(jnp.bfloat16)
+            for at, to, count in ((0, 0, 128), (128, 192, 128), (256, 128, 64), (320, 320, 64)):
+                staged[slot, to:to + count, start:] = values[at:at + count]
+            if start:
+                staged[slot, :, :start] = jnp.zeros((C, start), jnp.bfloat16)
+            writes.append(pltpu.make_async_copy(staged.at[slot], out_ref.at[pair, member], written.at[slot]))
+            writes[-1].start()
+    for write in writes:
+        write.wait()
+
+
+def assemble(own_ref, packed_ref, kept, half):
     side = lax.axis_index("lon")
     block = order_block()
-    for tile in range(TILES + 1):
-        member, place = tile_place(tile, block)
-        lanes = pl.ds(pl.multiple_of(place * LANE, LANE), LANE)
-        for pair in range(PAIRS):
-            other[pair, member, :, lanes] = packed_ref[pair, :, tile * LANE:(tile + 1) * LANE]
-
-    def products(full):
-        writes = []
-        for pair in range(PAIRS):
-            index = lax.axis_index("lat") * PAIRS + pair
-            reads[pair].wait()
-            reads[PAIRS + pair].wait()
-            for member in range(2):
-                slot = (pair + member) % 2 * PAIRS + pair
-                start = 0 if member == full else MM // 2
-                order = MM - 1 - index if member else index
-                values = 0.0
-                for which, held in ((side, own_ref), (1 - side, other)):
-                    values += lax.dot_general(
-                        by_latitude(spectra, which, half, slot), held[pair, member, :, start:],
-                        (((0,), (0,)), ((), ())), preferred_element_type=jnp.float32)
-                degree = lax.broadcasted_iota(jnp.int32, values.shape, 1) + start
-                values = jnp.where(degree >= order, values, 0.0).astype(jnp.bfloat16)
-                for at, to, count in ((0, 0, 128), (128, 192, 128), (256, 128, 64), (320, 320, 64)):
-                    staged[slot, to:to + count, start:] = values[at:at + count]
-                if start:
-                    staged[slot, :, :start] = jnp.zeros((C, start), jnp.bfloat16)
-                writes.append(pltpu.make_async_copy(staged.at[slot], out_ref.at[pair, member], written.at[slot]))
-                writes[-1].start()
-        for write in writes:
-            write.wait()
-
-    for full in range(2):
-        pl.when((block < TILES // 2) == (full == 0))(lambda full=full: products(full))
-
-
-def by_latitude(spectra, which, half, slot):
-    pieces = []
-    for at in range(half // 16):
-        first, second = (LISTED.index(2 * index) // 2 for index in (at, at + half // 16))
-        start = pl.multiple_of(16 * jnp.where(which == 0, first, second), 16)
-        pieces.append(spectra[pl.ds(start, 16), slot * C:(slot + 1) * C])
-    return jnp.concatenate(pieces, axis=0)
+    mine = pl.ds(pl.multiple_of(side * half, half), half)
+    theirs = pl.ds(pl.multiple_of((1 - side) * half, half), half)
+    for pair in range(PAIRS):
+        for member in range(2):
+            start = member * SECOND_FROM
+            kept[pair, member, mine, start:] = own_ref[pair, member, :, start:]
+            kept[pair, member, theirs, start:start + LANE] = jnp.zeros((half, LANE), jnp.bfloat16)
+        for tile in range(TILES + 1):
+            member, place = tile_place(tile, block)
+            lanes = pl.ds(pl.multiple_of(place * LANE, LANE), LANE)
+            kept[pair, member, theirs, lanes] = packed_ref[pair, :, tile * LANE:(tile + 1) * LANE]
+
+
+def by_latitude(spectra, slot):
+    starts = [LATS * LISTED.index(lat) for lat in range(0, OWNERS, 2)]
+    return jnp.concatenate([spectra[start:start + 16, slot * C:(slot + 1) * C] for start in starts], axis=0)
 
 
 def contract(spectra, legendre, packed):
-    half = legendre.shape[2]
+    rows = spectra.shape[0]
     spectra = pltpu.with_memory_space_constraint(spectra, pltpu.HBM)
     return pl.pallas_call(
         contract_kernel,
@@ -329,14 +332,14 @@
         out_specs=IN_HBM,
         out_shape=pltpu.HBM((PAIRS, 2, C, MM), jnp.bfloat16),
         scratch_shapes=[
-            pltpu.VMEM((PAIRS, 2, half, MM), jnp.bfloat16),
+            pltpu.VMEM((PAIRS, 2, rows, MM), jnp.bfloat16),
             pltpu.VMEM(spectra.shape, jnp.bfloat16),
             pltpu.VMEM((2 * PAIRS, C, MM), jnp.bfloat16),
             pltpu.SemaphoreType.DMA((2 * PAIRS,)),
             pltpu.SemaphoreType.DMA((2 * PAIRS,)),
         ],
         compiler_params=pltpu.CompilerParams(vmem_limit_bytes=MEDIUM),
-        cost_estimate=pl.CostEstimate(flops=8 * PAIRS * half * C * MM, bytes_accessed=8 * MIB, transcendentals=0),
+        cost_estimate=pl.CostEstimate(flops=4 * PAIRS * rows * C * MM, bytes_accessed=8 * MIB, transcendentals=0),
     )(spectra, legendre, packed)
 
 

time: 79.9 us -> 79.6 us (level)
  no operation moved by 1% of the time
where the time goes in v5:
time: 79.6 us; the launch traced here: 79.3 us
  waiting for transfers between devices  38.7 us (49%)
  Pallas kernels  19 us (24%)
  starting transfers between devices  18 us (23%)
  local copies, waits for them, and re-layouts  3.33 us (4%)
    ppermute x1, waiting for transfers between devices, shards(): packed = lax.ppermute(packed, 'lon', swap)  29.3 us
    all_to_all x1, starting transfers between devices, shards(): lax.all_to_all(spectra, ALL, split_axis=0, concat_axis=0, tiled=True, axi...  14.7 us
    all_to_all x1, waiting for transfers between devices, shards(): lax.all_to_all(spectra, ALL, split_axis=0, concat_axis=0, tiled=True, axi...  7 us
    pallas_call x1, Pallas kernels, transform(): pl.pallas_call(transform_kernel, in_specs=[IN_VMEM] * 8, out_specs=IN_HBM...  6.29 us
    pallas_call x1, Pallas kernels, encode_own(): pl.pallas_call(encode_own_kernel, in_specs=[IN_VMEM] + [IN_HBM] * 5, out_...  5.32 us
    pallas_call x1, Pallas kernels, contract(): pl.pallas_call(contract_kernel, in_specs=[IN_HBM, IN_VMEM, IN_VMEM], out_...  4.37 us
    pallas_call x1, Pallas kernels, first_lons(): pl.pallas_call(first_kernel, in_specs=[IN_VMEM] * 6, out_specs=IN_VMEM, o...  3.06 us
    ppermute x1, starting transfers between devices, shards(): received = [lax.ppermute(flat[:, :CHUNK], 'lon', swap)]  2.12 us
  transfers between devices with their start and end apart: 4, of which 4 were waited for; matrix products, arithmetic and copies ran while one was open for 3% of the time, Pallas kernels for 11%

profile of v5, /device:TPU:1, one launch (start us, length us, event | category | flops | bytes accessed | tf_op | source)
XLA Modules:
  0.0 79.3 jit_solution(2774399308802025378)
XLA Ops:
  0.0 1.1 %slice.8 = bf16[584,384]{1,0:T(8,128)(2,1)S(1)} slice(bf16[584,512]{1,0:T(8,128)(2,1)} %bitcast.21), slice={[0:584], [0:384]} | slice | bytes 897024 | tf_op jit(solution)/shard_map/slice | solution.py:353
  1.1 2.1 %collective-permute-start = (bf16[584,384]{1,0:T(8,128)(2,1)S(1)}, bf16[584,384]{1,0:T(8,128)(2,1)S(1)}, u32[]{:S(2)}, u32[]{:S(2)}) collective-permute-start(bf16[584,384]{1,0:T(8,128)(2,1)S(1)} %slice.8), channel_id=1, source_target_pairs={{0,1},{1,0},{2,3},{3,2},{4,5},{5,4},{6,7},{7,6},{8,9},{9,8},{10,11... | collective-permute-start | bytes 1345544 | tf_op jit(solution)/shard_map/ppermute | solution.py:353
  3.2 0.9 %slice.9 = bf16[584,128]{1,0:T(8,128)(2,1)S(1)} slice(bf16[584,512]{1,0:T(8,128)(2,1)} %bitcast.22), slice={[0:584], [384:512]} | slice | bytes 299008 | tf_op jit(solution)/shard_map/slice | solution.py:358
  4.1 1.2 %copy.15 = bf16[73,8,512]{2,0,1:T(8,128)(2,1)S(1)} copy(bf16[73,8,512]{2,1,0:T(8,128)(2,1)} %param.7) | data formatting | bytes 1196032 | tf_op args[0]
  5.4 5.3 %shard_map.73 = (bf16[8,512,384]{2,1,0:T(8,128)(2,1)S(1)}, bf16[4,256,640]{2,1,0:T(8,128)(2,1)}, bf16[73,384]{1,0:T(8,128)(2,1)S(1)}, f32[1,384]{1,0:T(1,128)S(1...) custom-call(bf16[8,73,512]{2,1,0:T(8,128)(2,1)S(1)} %bitcast.18, bf16[73,384]{1,0:T(8,128)(2,1)} %w1_hbm.1, ...), custom_call_target="tpu_custom_call" | custom-call | flops 1437597696 | bytes 1048576 | tf_op jit(solution)/shard_map/pallas_call | solution.py:175
  10.7 0.1 collective-permute-start.1
  10.8 1.9 %collective-permute-done = bf16[584,384]{1,0:T(8,128)(2,1)S(1)} collective-permute-done((bf16[584,384]{1,0:T(8,128)(2,1)S(1)}, bf16[584,384]{1,0:T(8,128)(2,1)S(1)}, u32[]{:S(2)}, u32[]{:S(2)}) %collective-permute-start) | collective-permute-done | bytes 448544 | tf_op jit(solution)/shard_map/ppermute | solution.py:353
  12.7 0.1 copy.16
  12.8 0.0 copy-start.1
  12.8 3.1 %shard_map.74.first_ref = bf16[2,8,384,384]{3,2,1,0:T(8,128)(2,1)S(1)} custom-call(bf16[8,73,384]{2,1,0:T(8,128)(2,1)S(1)} %bitcast.17, bf16[73,384]{1,0:T(8,128)(2,1)S(1)} %get-tuple-element.18.w1_ref, f32[1,384]{1,0:T(1,128)S(1)} %get-tuple-element.19.b1_ref, bf16[384,384]{1,0:T(8,128)(2,1)S(1)} %get-tuple-element.20.w2_ref, ...), custom_call_target="tpu_custom_call" | custom-call | flops 1078198272 | bytes 1048576 | tf_op jit(solution)/shard_map/pallas_call | solution.py:162
  15.8 0.5 collective-permute-done.1
  16.4 0.0 copy-done.1
  16.4 6.3 %shard_map.75 = bf16[16,2,2,8,3072]{4,3,2,1,0:T(8,128)(2,1)} custom-call(bf16[8,73,128]{2,1,0:T(8,128)(2,1)S(1)} %bitcast.19, bf16[73,384]{1,0:T(8,128)(2,1)S(1)} %get-tuple-element.18.w1_ref, f32[1,384]{1,0:T(1,128)S(1)} %get-tuple-element.19.b1_ref, bf16[384,384]{1,0:T(8,128)(2,1)S(1)} %get-tuple-element.20.w2_ref, f32[1,384]{1,0:T(1,128)S(1)} %get-tuple-element.21.b2_ref, ...), custom_call_target="tpu_custom_call" | custom-call | flops 3825205248 | bytes 4194304 | tf_op jit(solution)/shard_map/pallas_call | solution.py:252
  22.7 0.0 copy-start
  22.7 14.7 %all-to-all-start = ((bf16[64,8,3072]{2,1,0:T(8,128)(2,1)}), bf16[64,8,3072]{2,1,0:T(8,128)(2,1)}, u32[]{:S(2)}, u32[]{:S(2)}) async-start(bf16[64,8,3072]{2,1,0:T(8,128)(2,1)} %bitcast.20), calls=%async_computation | async-start | bytes 6291456 | tf_op jit(solution)/shard_map/all_to_all | solution.py:367
  37.4 1.1 %collective-permute-start.2 = (bf16[4,256,640]{2,1,0:T(8,128)(2,1)}, bf16[4,256,640]{2,1,0:T(8,128)(2,1)S(1)}, u32[]{:S(2)}, u32[]{:S(2)}) collective-permute-start(bf16[4,256,640]{2,1,0:T(8,128)(2,1)} %get-tuple-element.28), channel_id=1, source_target_pairs={{0,1},{1,0},{2,3},{3,2},{4,5},{5,4},{6,7},{7,6},{8,9},{9,8},{10,11... | collective-permute-start | bytes 3932168 | tf_op jit(solution)/shard_map/ppermute | solution.py:365
  38.5 29.3 %collective-permute-done.2.packed_ref = bf16[4,256,640]{2,1,0:T(8,128)(2,1)S(1)} collective-permute-done((bf16[4,256,640]{2,1,0:T(8,128)(2,1)}, bf16[4,256,640]{2,1,0:T(8,128)(2,1)S(1)}, u32[]{:S(2)}, u32[]{:S(2)}) %collective-permute-start.2) | collective-permute-done | bytes 1310752 | tf_op jit(solution)/shard_map/ppermute | solution.py:365
  67.8 7.0 %all-to-all-done = bf16[64,8,3072]{2,1,0:T(8,128)(2,1)} async-done(((bf16[64,8,3072]{2,1,0:T(8,128)(2,1)}), bf16[64,8,3072]{2,1,0:T(8,128)(2,1)}, u32[]{:S(2)}, u32[]{:S(2)}) %all-to-all-start) | async-done | bytes 3145760 | tf_op jit(solution)/shard_map/all_to_all | solution.py:367
  74.8 0.0 copy-done
  74.8 4.4 %shard_map.76 = bf16[4,2,384,512]{3,2,1,0:T(8,128)(2,1)} custom-call(bf16[512,3072]{1,0:T(8,128)(2,1)} %bitcast.7.spectra_ref, bf16[4,2,256,512]{3,2,1,0:T(8,128)(2,1)S(1)} %copy-done, bf16[4,256,640]{2,1,0:T(8,128)(2,1)S(1)} %collective-permute-done.2.packed_ref), custom_call_target="tpu_custom_call" | custom-call | flops 1610612736 | bytes 8388608 | tf_op jit(solution)/shard_map/pallas_call | solution.py:329
  (1 shorter events, 0.0 us)
Async XLA Ops:
  1.1 11.6 %collective-permute-start = (bf16[584,384]{1,0:T(8,128)(2,1)S(1)}, bf16[584,384]{1,0:T(8,128)(2,1)S(1)}, u32[]{:S(2)}, u32[]{:S(2)}) collective-permute-start(bf16[584,384]{1,0:T(8,128)(2,1)S(1)} %slice.8), channel_id=1, source_target_pairs={{0,1},{1,0},{2,3},{3,2},{4,5},{5,4},{6,7},{7,6},{8,9},{9,8},{10,11... | collective-permute-start | bytes 1345544 | tf_op jit(solution)/shard_map/ppermute | solution.py:353
  10.7 5.7 %collective-permute-start.1 = (bf16[584,128]{1,0:T(8,128)(2,1)S(1)}, bf16[584,128]{1,0:T(8,128)(2,1)S(1)}, u32[]{:S(2)}, u32[]{:S(2)}) collective-permute-start(bf16[584,128]{1,0:T(8,128)(2,1)S(1)} %slice.9), channel_id=1, source_target_pairs={{0,1},{1,0},{2,3},{3,2},{4,5},{5,4},{6,7},{7,6},{8,9},{9,8},{10,11... | collective-permute-start | bytes 448520 | tf_op jit(solution)/shard_map/ppermute | solution.py:359
  12.8 3.6 %copy-start.1 = (bf16[2,512,512]{2,1,0:T(8,128)(2,1)S(1)}, bf16[2,512,512]{2,1,0:T(8,128)(2,1)}, u32[]{:S(2)}) copy-start(bf16[2,512,512]{2,1,0:T(8,128)(2,1)} %constant.5.table_ref) | copy-start | bytes 3145732
  22.7 52.1 %copy-start = (bf16[4,2,256,512]{3,2,1,0:T(8,128)(2,1)S(1)}, bf16[4,2,256,512]{3,2,1,0:T(8,128)(2,1)}, u32[]{:S(2)}) copy-start(bf16[4,2,256,512]{3,2,1,0:T(8,128)(2,1)} %own_ref.1) | copy-start | bytes 6291460
  22.7 52.1 %all-to-all-start = ((bf16[64,8,3072]{2,1,0:T(8,128)(2,1)}), bf16[64,8,3072]{2,1,0:T(8,128)(2,1)}, u32[]{:S(2)}, u32[]{:S(2)}) async-start(bf16[64,8,3072]{2,1,0:T(8,128)(2,1)} %bitcast.20), calls=%async_computation | async-start | bytes 6291456 | tf_op jit(solution)/shard_map/all_to_all | solution.py:367
  37.4 30.4 %collective-permute-start.2 = (bf16[4,256,640]{2,1,0:T(8,128)(2,1)}, bf16[4,256,640]{2,1,0:T(8,128)(2,1)S(1)}, u32[]{:S(2)}, u32[]{:S(2)}) collective-permute-start(bf16[4,256,640]{2,1,0:T(8,128)(2,1)} %get-tuple-element.28), channel_id=1, source_target_pairs={{0,1},{1,0},{2,3},{3,2},{4,5},{5,4},{6,7},{7,6},{8,9},{9,8},{10,11... | collective-permute-start | bytes 3932168 | tf_op jit(solution)/shard_map/ppermute | solution.py:365

commit v6 on v5

--- a/solution.py
+++ b/solution.py
@@ -146,9 +146,8 @@
 
 
 def combine(own, theirs):
-    own, theirs = own.astype(jnp.float32), theirs.astype(jnp.float32)
-    sign = jnp.where(lax.axis_index("lon") == 0, 1.0, -1.0)
-    return (own + theirs).astype(jnp.bfloat16), (sign * (own - theirs)).astype(jnp.bfloat16)
+    sign = jnp.where(lax.axis_index("lon") == 0, 1.0, -1.0).astype(jnp.bfloat16)
+    return own + theirs, sign * (own - theirs)
 
 
 def first_kernel(x_ref, w1_ref, b1_ref, w2_ref, b2_ref, own_ref, parts_ref):

time: 79.6 us -> 78.8 us (0.990)
  starting transfers between devices: 18 us -> 17.2 us
  transfers between devices with their start and end apart: 4 -> 4, of which waited for: 4 -> 4; matrix products, arithmetic and copies ran while one was open for 3% -> 3% of each run, Pallas kernels for 11% -> 10%
where the time goes in v6:
time: 78.8 us; the launch traced here: 78.4 us
  waiting for transfers between devices  39.4 us (50%)
  Pallas kernels  18.4 us (23%)
  starting transfers between devices  17.2 us (22%)
  local copies, waits for them, and re-layouts  3.33 us (4%)
    ppermute x1, waiting for transfers between devices, shards(): packed = lax.ppermute(packed, 'lon', swap)  29.5 us
    all_to_all x1, starting transfers between devices, shards(): lax.all_to_all(spectra, ALL, split_axis=0, concat_axis=0, tiled=True, axi...  14.1 us
    all_to_all x1, waiting for transfers between devices, shards(): lax.all_to_all(spectra, ALL, split_axis=0, concat_axis=0, tiled=True, axi...  7 us
    pallas_call x1, Pallas kernels, transform(): pl.pallas_call(transform_kernel, in_specs=[IN_VMEM] * 8, out_specs=IN_HBM...  6.17 us
    pallas_call x1, Pallas kernels, encode_own(): pl.pallas_call(encode_own_kernel, in_specs=[IN_VMEM] + [IN_HBM] * 5, out_...  5.32 us
    pallas_call x1, Pallas kernels, contract(): pl.pallas_call(contract_kernel, in_specs=[IN_HBM, IN_VMEM, IN_VMEM], out_...  4.38 us
    pallas_call x1, Pallas kernels, first_lons(): pl.pallas_call(first_kernel, in_specs=[IN_VMEM] * 6, out_specs=IN_VMEM, o...  2.49 us
    ppermute x1, starting transfers between devices, shards(): received = [lax.ppermute(flat[:, :CHUNK], 'lon', swap)]  2.12 us
  transfers between devices with their start and end apart: 4, of which 4 were waited for; matrix products, arithmetic and copies ran while one was open for 3% of the time, Pallas kernels for 10%

profile of v6, /device:TPU:1, one launch (start us, length us, event | category | flops | bytes accessed | tf_op | source)
XLA Modules:
  0.0 78.4 jit_solution(2966001651058161541)
XLA Ops:
  0.0 1.1 %slice.8 = bf16[584,384]{1,0:T(8,128)(2,1)S(1)} slice(bf16[584,512]{1,0:T(8,128)(2,1)} %bitcast.21), slice={[0:584], [0:384]} | slice | bytes 897024 | tf_op jit(solution)/shard_map/slice | solution.py:352
  1.1 2.1 %collective-permute-start = (bf16[584,384]{1,0:T(8,128)(2,1)S(1)}, bf16[584,384]{1,0:T(8,128)(2,1)S(1)}, u32[]{:S(2)}, u32[]{:S(2)}) collective-permute-start(bf16[584,384]{1,0:T(8,128)(2,1)S(1)} %slice.8), channel_id=1, source_target_pairs={{0,1},{1,0},{2,3},{3,2},{4,5},{5,4},{6,7},{7,6},{8,9},{9,8},{10,11... | collective-permute-start | bytes 1345544 | tf_op jit(solution)/shard_map/ppermute | solution.py:352
  3.2 0.9 %slice.9 = bf16[584,128]{1,0:T(8,128)(2,1)S(1)} slice(bf16[584,512]{1,0:T(8,128)(2,1)} %bitcast.22), slice={[0:584], [384:512]} | slice | bytes 299008 | tf_op jit(solution)/shard_map/slice | solution.py:357
  4.1 1.2 %copy.15 = bf16[73,8,512]{2,0,1:T(8,128)(2,1)S(1)} copy(bf16[73,8,512]{2,1,0:T(8,128)(2,1)} %param.7) | data formatting | bytes 1196032 | tf_op args[0]
  5.4 5.3 %shard_map.73 = (bf16[8,512,384]{2,1,0:T(8,128)(2,1)S(1)}, bf16[4,256,640]{2,1,0:T(8,128)(2,1)}, bf16[73,384]{1,0:T(8,128)(2,1)S(1)}, f32[1,384]{1,0:T(1,128)S(1...) custom-call(bf16[8,73,512]{2,1,0:T(8,128)(2,1)S(1)} %bitcast.18, bf16[73,384]{1,0:T(8,128)(2,1)} %w1_hbm.1, ...), custom_call_target="tpu_custom_call" | custom-call | flops 1437597696 | bytes 1048576 | tf_op jit(solution)/shard_map/pallas_call | solution.py:174
  10.7 0.1 collective-permute-start.1
  10.8 1.9 %collective-permute-done = bf16[584,384]{1,0:T(8,128)(2,1)S(1)} collective-permute-done((bf16[584,384]{1,0:T(8,128)(2,1)S(1)}, bf16[584,384]{1,0:T(8,128)(2,1)S(1)}, u32[]{:S(2)}, u32[]{:S(2)}) %collective-permute-start) | collective-permute-done | bytes 448544 | tf_op jit(solution)/shard_map/ppermute | solution.py:352
  12.7 0.1 copy.16
  12.8 0.0 copy-start.1
  12.8 2.5 %shard_map.74.first_ref = bf16[2,8,384,384]{3,2,1,0:T(8,128)(2,1)S(1)} custom-call(bf16[8,73,384]{2,1,0:T(8,128)(2,1)S(1)} %bitcast.17, bf16[73,384]{1,0:T(8,128)(2,1)S(1)} %get-tuple-element.18.w1_ref, f32[1,384]{1,0:T(1,128)S(1)} %get-tuple-element.19.b1_ref, bf16[384,384]{1,0:T(8,128)(2,1)S(1)} %get-tuple-element.20.w2_ref, ...), custom_call_target="tpu_custom_call" | custom-call | flops 1078198272 | bytes 1048576 | tf_op jit(solution)/shard_map/pallas_call | solution.py:161
  15.3 1.1 %collective-permute-done.1 = bf16[584,128]{1,0:T(8,128)(2,1)S(1)} collective-permute-done((bf16[584,128]{1,0:T(8,128)(2,1)S(1)}, bf16[584,128]{1,0:T(8,128)(2,1)S(1)}, u32[]{:S(2)}, u32[]{:S(2)}) %collective-permute-start.1) | collective-permute-done | bytes 149536 | tf_op jit(solution)/shard_map/ppermute | solution.py:358
  16.4 0.0 copy-done.1
  16.4 6.2 %shard_map.75 = bf16[16,2,2,8,3072]{4,3,2,1,0:T(8,128)(2,1)} custom-call(bf16[8,73,128]{2,1,0:T(8,128)(2,1)S(1)} %bitcast.19, bf16[73,384]{1,0:T(8,128)(2,1)S(1)} %get-tuple-element.18.w1_ref, f32[1,384]{1,0:T(1,128)S(1)} %get-tuple-element.19.b1_ref, bf16[384,384]{1,0:T(8,128)(2,1)S(1)} %get-tuple-element.20.w2_ref, f32[1,384]{1,0:T(1,128)S(1)} %get-tuple-element.21.b2_ref, ...), custom_call_target="tpu_custom_call" | custom-call | flops 3825205248 | bytes 4194304 | tf_op jit(solution)/shard_map/pallas_call | solution.py:251
  22.6 0.0 copy-start
  22.6 14.1 %all-to-all-start = ((bf16[64,8,3072]{2,1,0:T(8,128)(2,1)}), bf16[64,8,3072]{2,1,0:T(8,128)(2,1)}, u32[]{:S(2)}, u32[]{:S(2)}) async-start(bf16[64,8,3072]{2,1,0:T(8,128)(2,1)} %bitcast.20), calls=%async_computation | async-start | bytes 6291456 | tf_op jit(solution)/shard_map/all_to_all | solution.py:366
  36.6 0.9 %collective-permute-start.2 = (bf16[4,256,640]{2,1,0:T(8,128)(2,1)}, bf16[4,256,640]{2,1,0:T(8,128)(2,1)S(1)}, u32[]{:S(2)}, u32[]{:S(2)}) collective-permute-start(bf16[4,256,640]{2,1,0:T(8,128)(2,1)} %get-tuple-element.28), channel_id=1, source_target_pairs={{0,1},{1,0},{2,3},{3,2},{4,5},{5,4},{6,7},{7,6},{8,9},{9,8},{10,11... | collective-permute-start | bytes 3932168 | tf_op jit(solution)/shard_map/ppermute | solution.py:364
  37.6 29.5 %collective-permute-done.2.packed_ref = bf16[4,256,640]{2,1,0:T(8,128)(2,1)S(1)} collective-permute-done((bf16[4,256,640]{2,1,0:T(8,128)(2,1)}, bf16[4,256,640]{2,1,0:T(8,128)(2,1)S(1)}, u32[]{:S(2)}, u32[]{:S(2)}) %collective-permute-start.2) | collective-permute-done | bytes 1310752 | tf_op jit(solution)/shard_map/ppermute | solution.py:364
  67.0 7.0 %all-to-all-done = bf16[64,8,3072]{2,1,0:T(8,128)(2,1)} async-done(((bf16[64,8,3072]{2,1,0:T(8,128)(2,1)}), bf16[64,8,3072]{2,1,0:T(8,128)(2,1)}, u32[]{:S(2)}, u32[]{:S(2)}) %all-to-all-start) | async-done | bytes 3145760 | tf_op jit(solution)/shard_map/all_to_all | solution.py:366
  74.0 0.0 copy-done
  74.1 4.4 %shard_map.76 = bf16[4,2,384,512]{3,2,1,0:T(8,128)(2,1)} custom-call(bf16[512,3072]{1,0:T(8,128)(2,1)} %bitcast.7.spectra_ref, bf16[4,2,256,512]{3,2,1,0:T(8,128)(2,1)S(1)} %copy-done, bf16[4,256,640]{2,1,0:T(8,128)(2,1)S(1)} %collective-permute-done.2.packed_ref), custom_call_target="tpu_custom_call" | custom-call | flops 1610612736 | bytes 8388608 | tf_op jit(solution)/shard_map/pallas_call | solution.py:328
  (1 shorter events, 0.0 us)
Async XLA Ops:
  1.1 11.6 %collective-permute-start = (bf16[584,384]{1,0:T(8,128)(2,1)S(1)}, bf16[584,384]{1,0:T(8,128)(2,1)S(1)}, u32[]{:S(2)}, u32[]{:S(2)}) collective-permute-start(bf16[584,384]{1,0:T(8,128)(2,1)S(1)} %slice.8), channel_id=1, source_target_pairs={{0,1},{1,0},{2,3},{3,2},{4,5},{5,4},{6,7},{7,6},{8,9},{9,8},{10,11... | collective-permute-start | bytes 1345544 | tf_op jit(solution)/shard_map/ppermute | solution.py:352
  10.7 5.7 %collective-permute-start.1 = (bf16[584,128]{1,0:T(8,128)(2,1)S(1)}, bf16[584,128]{1,0:T(8,128)(2,1)S(1)}, u32[]{:S(2)}, u32[]{:S(2)}) collective-permute-start(bf16[584,128]{1,0:T(8,128)(2,1)S(1)} %slice.9), channel_id=1, source_target_pairs={{0,1},{1,0},{2,3},{3,2},{4,5},{5,4},{6,7},{7,6},{8,9},{9,8},{10,11... | collective-permute-start | bytes 448520 | tf_op jit(solution)/shard_map/ppermute | solution.py:358
  12.8 3.6 %copy-start.1 = (bf16[2,512,512]{2,1,0:T(8,128)(2,1)S(1)}, bf16[2,512,512]{2,1,0:T(8,128)(2,1)}, u32[]{:S(2)}) copy-start(bf16[2,512,512]{2,1,0:T(8,128)(2,1)} %constant.5.table_ref) | copy-start | bytes 3145732
  22.6 51.5 %copy-start = (bf16[4,2,256,512]{3,2,1,0:T(8,128)(2,1)S(1)}, bf16[4,2,256,512]{3,2,1,0:T(8,128)(2,1)}, u32[]{:S(2)}) copy-start(bf16[4,2,256,512]{3,2,1,0:T(8,128)(2,1)} %own_ref.1) | copy-start | bytes 6291460
  22.6 51.5 %all-to-all-start = ((bf16[64,8,3072]{2,1,0:T(8,128)(2,1)}), bf16[64,8,3072]{2,1,0:T(8,128)(2,1)}, u32[]{:S(2)}, u32[]{:S(2)}) async-start(bf16[64,8,3072]{2,1,0:T(8,128)(2,1)} %bitcast.20), calls=%async_computation | async-start | bytes 6291456 | tf_op jit(solution)/shard_map/all_to_all | solution.py:366
  36.6 30.4 %collective-permute-start.2 = (bf16[4,256,640]{2,1,0:T(8,128)(2,1)}, bf16[4,256,640]{2,1,0:T(8,128)(2,1)S(1)}, u32[]{:S(2)}, u32[]{:S(2)}) collective-permute-start(bf16[4,256,640]{2,1,0:T(8,128)(2,1)} %get-tuple-element.28), channel_id=1, source_target_pairs={{0,1},{1,0},{2,3},{3,2},{4,5},{5,4},{6,7},{7,6},{8,9},{9,8},{10,11... | collective-permute-start | bytes 3932168 | tf_op jit(solution)/shard_map/ppermute | solution.py:364

commit v7 on v6

--- a/solution.py
+++ b/solution.py
@@ -211,7 +211,7 @@
             slot = parity * PAIRS + pair
             copies.append(pltpu.make_async_copy(
                 staged.at[block, pair],
-                out_ref.at[:, BITS.index(bit), :, :, slot * C:(slot + 1) * C],
+                out_ref.at[:, BITS.index(bit), :, slot * C:(slot + 1) * C],
                 sems.at[block, pair],
             ))
             copies[-1].start()
@@ -244,7 +244,7 @@
         real = pltpu.roll(real, 64, 1)
     lane = lax.broadcasted_iota(jnp.int32, real.shape, 1)
     for at, piece in enumerate((held[0, 0], held[1, 0], jnp.where(lane < 64, real, imag))):
-        staged[:, :, :, at * LANE:(at + 1) * LANE] = piece.reshape(-1, 2, LATS, LANE).astype(jnp.bfloat16)
+        staged[:, :, at * LANE:(at + 1) * LANE] = piece.astype(jnp.bfloat16).reshape(-1, 2 * LATS, LANE)
 
 
 def transform(x, encoder, own, first, table):
@@ -252,11 +252,11 @@
         transform_kernel,
         in_specs=[IN_VMEM] * 8,
         out_specs=IN_HBM,
-        out_shape=pltpu.HBM((OWNERS // 4, 2, 2, LATS, 2 * PAIRS * C), jnp.bfloat16),
+        out_shape=pltpu.HBM((OWNERS // 4, 2, 2 * LATS, 2 * PAIRS * C), jnp.bfloat16),
         scratch_shapes=[
             pltpu.VMEM((2, LATS, x.shape[2], C), jnp.bfloat16),
             pltpu.VMEM((4, PAIRS, 2, 2, OWNERS // 2 * LATS, LANE), jnp.float32),
-            pltpu.VMEM((4, PAIRS, OWNERS // 4, 2, LATS, C), jnp.bfloat16),
+            pltpu.VMEM((4, PAIRS, OWNERS // 4, 2 * LATS, C), jnp.bfloat16),
             pltpu.SemaphoreType.DMA((4, PAIRS)),
         ],
         compiler_params=pltpu.CompilerParams(vmem_limit_bytes=MEDIUM),

time: 78.8 us -> 78.8 us (level)
  no operation moved by 1% of the time
where the time goes in v7:
time: 78.8 us; the launch traced here: 78.4 us
  waiting for transfers between devices  39.4 us (50%)
  Pallas kernels  18.4 us (23%)
  starting transfers between devices  17.2 us (22%)
  local copies, waits for them, and re-layouts  3.33 us (4%)
    ppermute x1, waiting for transfers between devices, shards(): packed = lax.ppermute(packed, 'lon', swap)  29.5 us
    all_to_all x1, starting transfers between devices, shards(): lax.all_to_all(spectra, ALL, split_axis=0, concat_axis=0, tiled=True, axi...  14.1 us
    all_to_all x1, waiting for transfers between devices, shards(): lax.all_to_all(spectra, ALL, split_axis=0, concat_axis=0, tiled=True, axi...  7 us
    pallas_call x1, Pallas kernels, transform(): pl.pallas_call(transform_kernel, in_specs=[IN_VMEM] * 8, out_specs=IN_HBM...  6.17 us
    pallas_call x1, Pallas kernels, encode_own(): pl.pallas_call(encode_own_kernel, in_specs=[IN_VMEM] + [IN_HBM] * 5, out_...  5.32 us
    pallas_call x1, Pallas kernels, contract(): pl.pallas_call(contract_kernel, in_specs=[IN_HBM, IN_VMEM, IN_VMEM], out_...  4.38 us
    pallas_call x1, Pallas kernels, first_lons(): pl.pallas_call(first_kernel, in_specs=[IN_VMEM] * 6, out_specs=IN_VMEM, o...  2.49 us
    ppermute x1, starting transfers between devices, shards(): received = [lax.ppermute(flat[:, :CHUNK], 'lon', swap)]  2.12 us
  transfers between devices with their start and end apart: 4, of which 4 were waited for; matrix products, arithmetic and copies ran while one was open for 3% of the time, Pallas kernels for 10%

profile of v7, /device:TPU:1, one launch (start us, length us, event | category | flops | bytes accessed | tf_op | source)
XLA Modules:
  0.0 78.4 jit_solution(2966001651058161541)
XLA Ops:
  0.0 1.1 %slice.8 = bf16[584,384]{1,0:T(8,128)(2,1)S(1)} slice(bf16[584,512]{1,0:T(8,128)(2,1)} %bitcast.21), slice={[0:584], [0:384]} | slice | bytes 897024 | tf_op jit(solution)/shard_map/slice | solution.py:352
  1.1 2.1 %collective-permute-start = (bf16[584,384]{1,0:T(8,128)(2,1)S(1)}, bf16[584,384]{1,0:T(8,128)(2,1)S(1)}, u32[]{:S(2)}, u32[]{:S(2)}) collective-permute-start(bf16[584,384]{1,0:T(8,128)(2,1)S(1)} %slice.8), channel_id=1, source_target_pairs={{0,1},{1,0},{2,3},{3,2},{4,5},{5,4},{6,7},{7,6},{8,9},{9,8},{10,11... | collective-permute-start | bytes 1345544 | tf_op jit(solution)/shard_map/ppermute | solution.py:352
  3.2 0.9 %slice.9 = bf16[584,128]{1,0:T(8,128)(2,1)S(1)} slice(bf16[584,512]{1,0:T(8,128)(2,1)} %bitcast.22), slice={[0:584], [384:512]} | slice | bytes 299008 | tf_op jit(solution)/shard_map/slice | solution.py:357
  4.1 1.2 %copy.15 = bf16[73,8,512]{2,0,1:T(8,128)(2,1)S(1)} copy(bf16[73,8,512]{2,1,0:T(8,128)(2,1)} %param.7) | data formatting | bytes 1196032 | tf_op args[0]
  5.4 5.3 %shard_map.73 = (bf16[8,512,384]{2,1,0:T(8,128)(2,1)S(1)}, bf16[4,256,640]{2,1,0:T(8,128)(2,1)}, bf16[73,384]{1,0:T(8,128)(2,1)S(1)}, f32[1,384]{1,0:T(1,128)S(1...) custom-call(bf16[8,73,512]{2,1,0:T(8,128)(2,1)S(1)} %bitcast.18, bf16[73,384]{1,0:T(8,128)(2,1)} %w1_hbm.1, ...), custom_call_target="tpu_custom_call" | custom-call | flops 1437597696 | bytes 1048576 | tf_op jit(solution)/shard_map/pallas_call | solution.py:174
  10.7 0.1 collective-permute-start.1
  10.8 1.9 %collective-permute-done = bf16[584,384]{1,0:T(8,128)(2,1)S(1)} collective-permute-done((bf16[584,384]{1,0:T(8,128)(2,1)S(1)}, bf16[584,384]{1,0:T(8,128)(2,1)S(1)}, u32[]{:S(2)}, u32[]{:S(2)}) %collective-permute-start) | collective-permute-done | bytes 448544 | tf_op jit(solution)/shard_map/ppermute | solution.py:352
  12.7 0.1 copy.16
  12.8 0.0 copy-start.1
  12.8 2.5 %shard_map.74.first_ref = bf16[2,8,384,384]{3,2,1,0:T(8,128)(2,1)S(1)} custom-call(bf16[8,73,384]{2,1,0:T(8,128)(2,1)S(1)} %bitcast.17, bf16[73,384]{1,0:T(8,128)(2,1)S(1)} %get-tuple-element.18.w1_ref, f32[1,384]{1,0:T(1,128)S(1)} %get-tuple-element.19.b1_ref, bf16[384,384]{1,0:T(8,128)(2,1)S(1)} %get-tuple-element.20.w2_ref, ...), custom_call_target="tpu_custom_call" | custom-call | flops 1078198272 | bytes 1048576 | tf_op jit(solution)/shard_map/pallas_call | solution.py:161
  15.3 1.1 %collective-permute-done.1 = bf16[584,128]{1,0:T(8,128)(2,1)S(1)} collective-permute-done((bf16[584,128]{1,0:T(8,128)(2,1)S(1)}, bf16[584,128]{1,0:T(8,128)(2,1)S(1)}, u32[]{:S(2)}, u32[]{:S(2)}) %collective-permute-start.1) | collective-permute-done | bytes 149536 | tf_op jit(solution)/shard_map/ppermute | solution.py:358
  16.4 0.0 copy-done.1
  16.4 6.2 %shard_map.75 = bf16[16,2,16,3072]{3,2,1,0:T(8,128)(2,1)} custom-call(bf16[8,73,128]{2,1,0:T(8,128)(2,1)S(1)} %bitcast.19, bf16[73,384]{1,0:T(8,128)(2,1)S(1)} %get-tuple-element.18.w1_ref, f32[1,384]{1,0:T(1,128)S(1)} %get-tuple-element.19.b1_ref, bf16[384,384]{1,0:T(8,128)(2,1)S(1)} %get-tuple-element.20.w2_ref, f32[1,384]{1,0:T(1,128)S(1)} %get-tuple-element.21.b2_ref, ...), custom_call_target="tpu_custom_call" | custom-call | flops 3825205248 | bytes 4194304 | tf_op jit(solution)/shard_map/pallas_call | solution.py:251
  22.6 0.0 copy-start
  22.6 14.1 %all-to-all-start = ((bf16[64,8,3072]{2,1,0:T(8,128)(2,1)}), bf16[64,8,3072]{2,1,0:T(8,128)(2,1)}, u32[]{:S(2)}, u32[]{:S(2)}) async-start(bf16[64,8,3072]{2,1,0:T(8,128)(2,1)} %bitcast.20), calls=%async_computation | async-start | bytes 6291456 | tf_op jit(solution)/shard_map/all_to_all | solution.py:366
  36.6 0.9 %collective-permute-start.2 = (bf16[4,256,640]{2,1,0:T(8,128)(2,1)}, bf16[4,256,640]{2,1,0:T(8,128)(2,1)S(1)}, u32[]{:S(2)}, u32[]{:S(2)}) collective-permute-start(bf16[4,256,640]{2,1,0:T(8,128)(2,1)} %get-tuple-element.28), channel_id=1, source_target_pairs={{0,1},{1,0},{2,3},{3,2},{4,5},{5,4},{6,7},{7,6},{8,9},{9,8},{10,11... | collective-permute-start | bytes 3932168 | tf_op jit(solution)/shard_map/ppermute | solution.py:364
  37.6 29.5 %collective-permute-done.2.packed_ref = bf16[4,256,640]{2,1,0:T(8,128)(2,1)S(1)} collective-permute-done((bf16[4,256,640]{2,1,0:T(8,128)(2,1)}, bf16[4,256,640]{2,1,0:T(8,128)(2,1)S(1)}, u32[]{:S(2)}, u32[]{:S(2)}) %collective-permute-start.2) | collective-permute-done | bytes 1310752 | tf_op jit(solution)/shard_map/ppermute | solution.py:364
  67.0 7.0 %all-to-all-done = bf16[64,8,3072]{2,1,0:T(8,128)(2,1)} async-done(((bf16[64,8,3072]{2,1,0:T(8,128)(2,1)}), bf16[64,8,3072]{2,1,0:T(8,128)(2,1)}, u32[]{:S(2)}, u32[]{:S(2)}) %all-to-all-start) | async-done | bytes 3145760 | tf_op jit(solution)/shard_map/all_to_all | solution.py:366
  74.0 0.0 copy-done
  74.1 4.4 %shard_map.76 = bf16[4,2,384,512]{3,2,1,0:T(8,128)(2,1)} custom-call(bf16[512,3072]{1,0:T(8,128)(2,1)} %bitcast.7.spectra_ref, bf16[4,2,256,512]{3,2,1,0:T(8,128)(2,1)S(1)} %copy-done, bf16[4,256,640]{2,1,0:T(8,128)(2,1)S(1)} %collective-permute-done.2.packed_ref), custom_call_target="tpu_custom_call" | custom-call | flops 1610612736 | bytes 8388608 | tf_op jit(solution)/shard_map/pallas_call | solution.py:328
  (1 shorter events, 0.0 us)
Async XLA Ops:
  1.1 11.6 %collective-permute-start = (bf16[584,384]{1,0:T(8,128)(2,1)S(1)}, bf16[584,384]{1,0:T(8,128)(2,1)S(1)}, u32[]{:S(2)}, u32[]{:S(2)}) collective-permute-start(bf16[584,384]{1,0:T(8,128)(2,1)S(1)} %slice.8), channel_id=1, source_target_pairs={{0,1},{1,0},{2,3},{3,2},{4,5},{5,4},{6,7},{7,6},{8,9},{9,8},{10,11... | collective-permute-start | bytes 1345544 | tf_op jit(solution)/shard_map/ppermute | solution.py:352
  10.7 5.7 %collective-permute-start.1 = (bf16[584,128]{1,0:T(8,128)(2,1)S(1)}, bf16[584,128]{1,0:T(8,128)(2,1)S(1)}, u32[]{:S(2)}, u32[]{:S(2)}) collective-permute-start(bf16[584,128]{1,0:T(8,128)(2,1)S(1)} %slice.9), channel_id=1, source_target_pairs={{0,1},{1,0},{2,3},{3,2},{4,5},{5,4},{6,7},{7,6},{8,9},{9,8},{10,11... | collective-permute-start | bytes 448520 | tf_op jit(solution)/shard_map/ppermute | solution.py:358
  12.8 3.6 %copy-start.1 = (bf16[2,512,512]{2,1,0:T(8,128)(2,1)S(1)}, bf16[2,512,512]{2,1,0:T(8,128)(2,1)}, u32[]{:S(2)}) copy-start(bf16[2,512,512]{2,1,0:T(8,128)(2,1)} %constant.5.table_ref) | copy-start | bytes 3145732
  22.6 51.5 %copy-start = (bf16[4,2,256,512]{3,2,1,0:T(8,128)(2,1)S(1)}, bf16[4,2,256,512]{3,2,1,0:T(8,128)(2,1)}, u32[]{:S(2)}) copy-start(bf16[4,2,256,512]{3,2,1,0:T(8,128)(2,1)} %own_ref.1) | copy-start | bytes 6291460
  22.6 51.5 %all-to-all-start = ((bf16[64,8,3072]{2,1,0:T(8,128)(2,1)}), bf16[64,8,3072]{2,1,0:T(8,128)(2,1)}, u32[]{:S(2)}, u32[]{:S(2)}) async-start(bf16[64,8,3072]{2,1,0:T(8,128)(2,1)} %bitcast.20), calls=%async_computation | async-start | bytes 6291456 | tf_op jit(solution)/shard_map/all_to_all | solution.py:366
  36.6 30.4 %collective-permute-start.2 = (bf16[4,256,640]{2,1,0:T(8,128)(2,1)}, bf16[4,256,640]{2,1,0:T(8,128)(2,1)S(1)}, u32[]{:S(2)}, u32[]{:S(2)}) collective-permute-start(bf16[4,256,640]{2,1,0:T(8,128)(2,1)} %get-tuple-element.28), channel_id=1, source_target_pairs={{0,1},{1,0},{2,3},{3,2},{4,5},{5,4},{6,7},{7,6},{8,9},{9,8},{10,11... | collective-permute-start | bytes 3932168 | tf_op jit(solution)/shard_map/ppermute | solution.py:364

commit v8 on v7

--- a/solution.py
+++ b/solution.py
@@ -289,8 +289,11 @@
             values = lax.dot_general(
                 by_latitude(spectra, slot), kept[pair, member, :, start:],
                 (((0,), (0,)), ((), ())), preferred_element_type=jnp.float32)
-            degree = lax.broadcasted_iota(jnp.int32, values.shape, 1) + start
-            values = jnp.where(degree >= order, values, 0.0).astype(jnp.bfloat16)
+            degree = lax.broadcasted_iota(jnp.int32, (C, SECOND_FROM), 1) + start
+            kept_values = jnp.where(degree >= order, values[:, :SECOND_FROM], 0.0).astype(jnp.bfloat16)
+            if member == 0:
+                kept_values = jnp.concatenate([kept_values, values[:, SECOND_FROM:].astype(jnp.bfloat16)], axis=1)
+            values = kept_values
             for at, to, count in ((0, 0, 128), (128, 192, 128), (256, 128, 64), (320, 320, 64)):
                 staged[slot, to:to + count, start:] = values[at:at + count]
             if start:

time: 78.8 us -> 78.8 us (level)
  no operation moved by 1% of the time
where the time goes in v8:
time: 78.8 us; the launch traced here: 78.4 us
  waiting for transfers between devices  39.4 us (50%)
  Pallas kernels  18.4 us (23%)
  starting transfers between devices  17.2 us (22%)
  local copies, waits for them, and re-layouts  3.33 us (4%)
    ppermute x1, waiting for transfers between devices, shards(): packed = lax.ppermute(packed, 'lon', swap)  29.5 us
    all_to_all x1, starting transfers between devices, shards(): lax.all_to_all(spectra, ALL, split_axis=0, concat_axis=0, tiled=True, axi...  14.1 us
    all_to_all x1, waiting for transfers between devices, shards(): lax.all_to_all(spectra, ALL, split_axis=0, concat_axis=0, tiled=True, axi...  7 us
    pallas_call x1, Pallas kernels, transform(): pl.pallas_call(transform_kernel, in_specs=[IN_VMEM] * 8, out_specs=IN_HBM...  6.17 us
    pallas_call x1, Pallas kernels, encode_own(): pl.pallas_call(encode_own_kernel, in_specs=[IN_VMEM] + [IN_HBM] * 5, out_...  5.32 us
    pallas_call x1, Pallas kernels, contract(): pl.pallas_call(contract_kernel, in_specs=[IN_HBM, IN_VMEM, IN_VMEM], out_...  4.39 us
    pallas_call x1, Pallas kernels, first_lons(): pl.pallas_call(first_kernel, in_specs=[IN_VMEM] * 6, out_specs=IN_VMEM, o...  2.49 us
    ppermute x1, starting transfers between devices, shards(): received = [lax.ppermute(flat[:, :CHUNK], 'lon', swap)]  2.12 us
  transfers between devices with their start and end apart: 4, of which 4 were waited for; matrix products, arithmetic and copies ran while one was open for 3% of the time, Pallas kernels for 10%

profile of v8, /device:TPU:1, one launch (start us, length us, event | category | flops | bytes accessed | tf_op | source)
XLA Modules:
  0.0 78.4 jit_solution(16279969883300286707)
XLA Ops:
  0.0 1.1 %slice.8 = bf16[584,384]{1,0:T(8,128)(2,1)S(1)} slice(bf16[584,512]{1,0:T(8,128)(2,1)} %bitcast.21), slice={[0:584], [0:384]} | slice | bytes 897024 | tf_op jit(solution)/shard_map/slice | solution.py:355
  1.1 2.1 %collective-permute-start = (bf16[584,384]{1,0:T(8,128)(2,1)S(1)}, bf16[584,384]{1,0:T(8,128)(2,1)S(1)}, u32[]{:S(2)}, u32[]{:S(2)}) collective-permute-start(bf16[584,384]{1,0:T(8,128)(2,1)S(1)} %slice.8), channel_id=1, source_target_pairs={{0,1},{1,0},{2,3},{3,2},{4,5},{5,4},{6,7},{7,6},{8,9},{9,8},{10,11... | collective-permute-start | bytes 1345544 | tf_op jit(solution)/shard_map/ppermute | solution.py:355
  3.2 0.9 %slice.9 = bf16[584,128]{1,0:T(8,128)(2,1)S(1)} slice(bf16[584,512]{1,0:T(8,128)(2,1)} %bitcast.22), slice={[0:584], [384:512]} | slice | bytes 299008 | tf_op jit(solution)/shard_map/slice | solution.py:360
  4.1 1.2 %copy.15 = bf16[73,8,512]{2,0,1:T(8,128)(2,1)S(1)} copy(bf16[73,8,512]{2,1,0:T(8,128)(2,1)} %param.7) | data formatting | bytes 1196032 | tf_op args[0]
  5.4 5.3 %shard_map.73 = (bf16[8,512,384]{2,1,0:T(8,128)(2,1)S(1)}, bf16[4,256,640]{2,1,0:T(8,128)(2,1)}, bf16[73,384]{1,0:T(8,128)(2,1)S(1)}, f32[1,384]{1,0:T(1,128)S(1...) custom-call(bf16[8,73,512]{2,1,0:T(8,128)(2,1)S(1)} %bitcast.18, bf16[73,384]{1,0:T(8,128)(2,1)} %w1_hbm.1, ...), custom_call_target="tpu_custom_call" | custom-call | flops 1437597696 | bytes 1048576 | tf_op jit(solution)/shard_map/pallas_call | solution.py:174
  10.7 0.1 collective-permute-start.1
  10.8 1.9 %collective-permute-done = bf16[584,384]{1,0:T(8,128)(2,1)S(1)} collective-permute-done((bf16[584,384]{1,0:T(8,128)(2,1)S(1)}, bf16[584,384]{1,0:T(8,128)(2,1)S(1)}, u32[]{:S(2)}, u32[]{:S(2)}) %collective-permute-start) | collective-permute-done | bytes 448544 | tf_op jit(solution)/shard_map/ppermute | solution.py:355
  12.7 0.1 copy.16
  12.8 0.0 copy-start.1
  12.8 2.5 %shard_map.74.first_ref = bf16[2,8,384,384]{3,2,1,0:T(8,128)(2,1)S(1)} custom-call(bf16[8,73,384]{2,1,0:T(8,128)(2,1)S(1)} %bitcast.17, bf16[73,384]{1,0:T(8,128)(2,1)S(1)} %get-tuple-element.18.w1_ref, f32[1,384]{1,0:T(1,128)S(1)} %get-tuple-element.19.b1_ref, bf16[384,384]{1,0:T(8,128)(2,1)S(1)} %get-tuple-element.20.w2_ref, ...), custom_call_target="tpu_custom_call" | custom-call | flops 1078198272 | bytes 1048576 | tf_op jit(solution)/shard_map/pallas_call | solution.py:161
  15.3 1.1 %collective-permute-done.1 = bf16[584,128]{1,0:T(8,128)(2,1)S(1)} collective-permute-done((bf16[584,128]{1,0:T(8,128)(2,1)S(1)}, bf16[584,128]{1,0:T(8,128)(2,1)S(1)}, u32[]{:S(2)}, u32[]{:S(2)}) %collective-permute-start.1) | collective-permute-done | bytes 149536 | tf_op jit(solution)/shard_map/ppermute | solution.py:361
  16.4 0.0 copy-done.1
  16.4 6.2 %shard_map.75 = bf16[16,2,16,3072]{3,2,1,0:T(8,128)(2,1)} custom-call(bf16[8,73,128]{2,1,0:T(8,128)(2,1)S(1)} %bitcast.19, bf16[73,384]{1,0:T(8,128)(2,1)S(1)} %get-tuple-element.18.w1_ref, f32[1,384]{1,0:T(1,128)S(1)} %get-tuple-element.19.b1_ref, bf16[384,384]{1,0:T(8,128)(2,1)S(1)} %get-tuple-element.20.w2_ref, f32[1,384]{1,0:T(1,128)S(1)} %get-tuple-element.21.b2_ref, ...), custom_call_target="tpu_custom_call" | custom-call | flops 3825205248 | bytes 4194304 | tf_op jit(solution)/shard_map/pallas_call | solution.py:251
  22.6 0.0 copy-start
  22.6 14.1 %all-to-all-start = ((bf16[64,8,3072]{2,1,0:T(8,128)(2,1)}), bf16[64,8,3072]{2,1,0:T(8,128)(2,1)}, u32[]{:S(2)}, u32[]{:S(2)}) async-start(bf16[64,8,3072]{2,1,0:T(8,128)(2,1)} %bitcast.20), calls=%async_computation | async-start | bytes 6291456 | tf_op jit(solution)/shard_map/all_to_all | solution.py:369
  36.6 0.9 %collective-permute-start.2 = (bf16[4,256,640]{2,1,0:T(8,128)(2,1)}, bf16[4,256,640]{2,1,0:T(8,128)(2,1)S(1)}, u32[]{:S(2)}, u32[]{:S(2)}) collective-permute-start(bf16[4,256,640]{2,1,0:T(8,128)(2,1)} %get-tuple-element.28), channel_id=1, source_target_pairs={{0,1},{1,0},{2,3},{3,2},{4,5},{5,4},{6,7},{7,6},{8,9},{9,8},{10,11... | collective-permute-start | bytes 3932168 | tf_op jit(solution)/shard_map/ppermute | solution.py:367
  37.6 29.5 %collective-permute-done.2.packed_ref = bf16[4,256,640]{2,1,0:T(8,128)(2,1)S(1)} collective-permute-done((bf16[4,256,640]{2,1,0:T(8,128)(2,1)}, bf16[4,256,640]{2,1,0:T(8,128)(2,1)S(1)}, u32[]{:S(2)}, u32[]{:S(2)}) %collective-permute-start.2) | collective-permute-done | bytes 1310752 | tf_op jit(solution)/shard_map/ppermute | solution.py:367
  67.0 7.0 %all-to-all-done = bf16[64,8,3072]{2,1,0:T(8,128)(2,1)} async-done(((bf16[64,8,3072]{2,1,0:T(8,128)(2,1)}), bf16[64,8,3072]{2,1,0:T(8,128)(2,1)}, u32[]{:S(2)}, u32[]{:S(2)}) %all-to-all-start) | async-done | bytes 3145760 | tf_op jit(solution)/shard_map/all_to_all | solution.py:369
  74.0 0.0 copy-done
  74.1 4.4 %shard_map.76 = bf16[4,2,384,512]{3,2,1,0:T(8,128)(2,1)} custom-call(bf16[512,3072]{1,0:T(8,128)(2,1)} %bitcast.7.spectra_ref, bf16[4,2,256,512]{3,2,1,0:T(8,128)(2,1)S(1)} %copy-done, bf16[4,256,640]{2,1,0:T(8,128)(2,1)S(1)} %collective-permute-done.2.packed_ref), custom_call_target="tpu_custom_call" | custom-call | flops 1610612736 | bytes 8388608 | tf_op jit(solution)/shard_map/pallas_call | solution.py:331
  (1 shorter events, 0.0 us)
Async XLA Ops:
  1.1 11.6 %collective-permute-start = (bf16[584,384]{1,0:T(8,128)(2,1)S(1)}, bf16[584,384]{1,0:T(8,128)(2,1)S(1)}, u32[]{:S(2)}, u32[]{:S(2)}) collective-permute-start(bf16[584,384]{1,0:T(8,128)(2,1)S(1)} %slice.8), channel_id=1, source_target_pairs={{0,1},{1,0},{2,3},{3,2},{4,5},{5,4},{6,7},{7,6},{8,9},{9,8},{10,11... | collective-permute-start | bytes 1345544 | tf_op jit(solution)/shard_map/ppermute | solution.py:355
  10.7 5.7 %collective-permute-start.1 = (bf16[584,128]{1,0:T(8,128)(2,1)S(1)}, bf16[584,128]{1,0:T(8,128)(2,1)S(1)}, u32[]{:S(2)}, u32[]{:S(2)}) collective-permute-start(bf16[584,128]{1,0:T(8,128)(2,1)S(1)} %slice.9), channel_id=1, source_target_pairs={{0,1},{1,0},{2,3},{3,2},{4,5},{5,4},{6,7},{7,6},{8,9},{9,8},{10,11... | collective-permute-start | bytes 448520 | tf_op jit(solution)/shard_map/ppermute | solution.py:361
  12.8 3.6 %copy-start.1 = (bf16[2,512,512]{2,1,0:T(8,128)(2,1)S(1)}, bf16[2,512,512]{2,1,0:T(8,128)(2,1)}, u32[]{:S(2)}) copy-start(bf16[2,512,512]{2,1,0:T(8,128)(2,1)} %constant.5.table_ref) | copy-start | bytes 3145732
  22.6 51.5 %copy-start = (bf16[4,2,256,512]{3,2,1,0:T(8,128)(2,1)S(1)}, bf16[4,2,256,512]{3,2,1,0:T(8,128)(2,1)}, u32[]{:S(2)}) copy-start(bf16[4,2,256,512]{3,2,1,0:T(8,128)(2,1)} %own_ref.1) | copy-start | bytes 6291460
  22.6 51.5 %all-to-all-start = ((bf16[64,8,3072]{2,1,0:T(8,128)(2,1)}), bf16[64,8,3072]{2,1,0:T(8,128)(2,1)}, u32[]{:S(2)}, u32[]{:S(2)}) async-start(bf16[64,8,3072]{2,1,0:T(8,128)(2,1)} %bitcast.20), calls=%async_computation | async-start | bytes 6291456 | tf_op jit(solution)/shard_map/all_to_all | solution.py:369
  36.6 30.4 %collective-permute-start.2 = (bf16[4,256,640]{2,1,0:T(8,128)(2,1)}, bf16[4,256,640]{2,1,0:T(8,128)(2,1)S(1)}, u32[]{:S(2)}, u32[]{:S(2)}) collective-permute-start(bf16[4,256,640]{2,1,0:T(8,128)(2,1)} %get-tuple-element.28), channel_id=1, source_target_pairs={{0,1},{1,0},{2,3},{3,2},{4,5},{5,4},{6,7},{7,6},{8,9},{9,8},{10,11... | collective-permute-start | bytes 3932168 | tf_op jit(solution)/shard_map/ppermute | solution.py:367
